TPU v7x, 32 devices: a whole 2x2x4 slice. The times are simulated.
32 devices in a mesh: rep: 8 (over y, x, core), shard: 4 (over z).
Axes of the slice: x: 2, y: 2, z: 4, core: 2. Of those that a mesh axis runs over, the one named last changes fastest.
Arguments:
- prompt_x: bfloat16 [8, 8, 2048, 800], P(None, 'rep', 'shard'), may hold values from -6 to 6
- cont_x: bfloat16 [8, 32, 512, 800], P(None, ('rep', 'shard')), may hold values from -6 to 6
- cont_map: int32 [8, 32, 2], P(None, ('rep', 'shard')), may hold values from 0 to 7
- cont_start: int32 [8, 32, 2], P(None, ('rep', 'shard')), may hold values from 0 to 511, as said below
- w_in: float32 [800, 400], P('shard'), may hold values from -0.21875 to 0.21875
- w_conv: float32 [3, 400, 400], P(None, 'shard'), may hold values from -0.1875 to 0.1875
- w_out: float32 [400, 800], P('shard'), may hold values from -0.4375 to 0.4375
- norm1_gain: float32 [800], replicated, may hold values from 0.1 to 1.9
- norm1_bias: float32 [800], replicated, may hold values from -3 to 3
- bias_in: float32 [400], replicated, may hold values from -3 to 3
- norm2_gain: float32 [400], replicated, may hold values from 0.1 to 1.9
- norm2_bias: float32 [400], replicated, may hold values from -3 to 3
- bias_conv: float32 [400], replicated, may hold values from -3 to 3
- norm3_gain: float32 [400], replicated, may hold values from 0.1 to 1.9
- norm3_bias: float32 [400], replicated, may hold values from -3 to 3
- bias_out: float32 [800], replicated, may hold values from -3 to 3
- prompt_cot: bfloat16 [8, 8, 2048, 800], P(None, 'rep', 'shard'), may hold values from -6 to 6
- cont_cot: bfloat16 [8, 32, 512, 800], P(None, ('rep', 'shard')), may hold values from -6 to 6
Outputs:
- prompt_out: bfloat16 [8, 8, 2048, 800], P(None, 'rep', 'shard')
- cont_out: bfloat16 [8, 32, 512, 800], P(None, ('rep', 'shard'))
- prompt_grad: float32 [8, 8, 2048, 800], P(None, 'rep', 'shard')
- cont_grad: float32 [8, 32, 512, 800], P(None, ('rep', 'shard'))
- grad_w_in: float32 [800, 400], P('shard')
- grad_w_conv: float32 [3, 400, 400], P(None, 'shard')
- grad_w_out: float32 [400, 800], P('shard')
- grad_norm1_gain: float32 [800], replicated
- grad_norm1_bias: float32 [800], replicated
- grad_bias_in: float32 [400], replicated
- grad_norm2_gain: float32 [400], replicated
- grad_norm2_bias: float32 [400], replicated
- grad_bias_conv: float32 [400], replicated
- grad_norm3_gain: float32 [400], replicated
- grad_norm3_bias: float32 [400], replicated
- grad_bias_out: float32 [800], replicated
Inputs may be any that keep to these rules, and one draw needn't show every extreme that they name: `cont_start`: in each buffer the 2 starts rise strictly and the first is 0; a continuation runs from its start to the next start or to the buffer's end. In the first buffer of every micro-batch the last start is 511.
All inputs are finite; a program needn't handle non-finite values.
Results may differ from a plain program's by a relative error of at most 0.0099.
Values may be sent and summed in bfloat16 or wider, within the bound.
No kernel may reach another device: no remote copies, remote signals or barrier semaphores. Data moves between devices by JAX's collectives and lax.ppermute only.
A program may use at most 256 MiB of HBM per device.

v0:
```python
import jax
import jax.numpy as jnp
from jax import lax
from jax.sharding import PartitionSpec as P

DILATION_STEP = 16


epsilon = 1e-05


def passed_along(x, axis, by):
    size = lax.axis_size(axis)
    pairs = [(i, i + by) for i in range(size) if 0 <= i + by < size]
    return lax.ppermute(x, axis, pairs)


def from_root(value, axis, source):
    kept = jnp.where(lax.axis_index(axis) == source, value, 0).astype(value.dtype)
    return lax.psum(kept, axis)


def norm_forward(values, gain, shift_by):
    center = values - jnp.mean(values, axis=-1, keepdims=True)
    scale = lax.rsqrt(jnp.mean(center * center, axis=-1, keepdims=True) + epsilon)
    normed = center * scale
    return (normed * gain + shift_by, normed, scale)


def norm_backward(grad, normed, scale, gain):
    scaled = grad * gain
    return scale * (
        scaled
        - jnp.mean(scaled, axis=-1, keepdims=True)
        - normed * jnp.mean(scaled * normed, axis=-1, keepdims=True)
    )


def silu_slope(values):
    sigma = jax.nn.sigmoid(values)
    return sigma * (1.0 + values * (1.0 - sigma))


def row_total(values):
    return jnp.sum(values, axis=(0, 1))


def layout(cont_start, cont_map, continuation_row_block, receptive_width):
    starts = cont_start[:, 0]
    owners = cont_map[:, 0]
    row_ids = jnp.arange(continuation_row_block, dtype=jnp.int32)
    member = jnp.sum((row_ids[None, :, None] >= starts[:, None, :]).astype(jnp.int32), axis=-1) - 1
    picked = member[:, :, None] == jnp.arange(starts.shape[1], dtype=jnp.int32)[None, None, :]
    begin = jnp.sum(jnp.where(picked, starts[:, None, :], 0), axis=-1)
    owning_prompt = jnp.sum(jnp.where(picked, owners[:, None, :], 0), axis=-1)
    row_position = row_ids[None, :] - begin
    causal_masks = [
        row_position >= kernel_tap_index * DILATION_STEP for kernel_tap_index in range(3)
    ]
    indices = [
        owning_prompt * receptive_width
        + jnp.clip(
            receptive_width + row_position - kernel_tap_index * DILATION_STEP,
            0,
            receptive_width - 1,
        )
        for kernel_tap_index in range(3)
    ]
    return (causal_masks, indices)


def pick_rows(table, row_index):
    return jax.vmap(lambda block, where_from: block[where_from])(table, row_index)


def on_device(
    prompt_x,
    cont_x,
    cont_map,
    cont_start,
    w_in,
    w_conv,
    w_out,
    norm1_gain,
    norm1_bias,
    bias_in,
    norm2_gain,
    norm2_bias,
    bias_conv,
    norm3_gain,
    norm3_bias,
    bias_out,
    prompt_cot,
    cont_cot,
):
    receptive_width = 2 * DILATION_STEP
    inner = w_conv.shape[2]
    prompt_row_block = prompt_x.shape[2]
    continuation_row_block = cont_x.shape[2]
    batches = prompt_x.shape[0]
    last_shard = lax.axis_size("shard") - 1
    low_in, low_conv, low_out = (
        lax.all_gather(w_in.astype(jnp.bfloat16), "shard", axis=0, tiled=True),
        lax.all_gather(w_conv.astype(jnp.bfloat16), "shard", axis=1, tiled=True),
        lax.all_gather(w_out.astype(jnp.bfloat16), "shard", axis=0, tiled=True),
    )
    rows_in = jnp.concatenate([prompt_x[:, 0], cont_x[:, 0]], axis=1).astype(jnp.float32)
    pre_one, normed_one, scale_one = norm_forward(rows_in, norm1_gain, norm1_bias)
    act_in = jax.nn.silu(pre_one).astype(jnp.bfloat16)
    hidden_in = (
        jnp.einsum("mrd,de->mre", act_in, low_in, preferred_element_type=jnp.float32) + bias_in
    )
    pre_two, normed_two, scale_two = norm_forward(hidden_in, norm2_gain, norm2_bias)
    act_mid = jax.nn.silu(pre_two).astype(jnp.bfloat16)
    prompt_act = act_mid[:, :prompt_row_block]
    cont_act = act_mid[:, prompt_row_block:]
    rim_rows = prompt_act[:, prompt_row_block - receptive_width :]
    halo_rows = passed_along(rim_rows, "shard", 1)
    tail_here = from_root(rim_rows, "shard", last_shard)
    tails = lax.all_gather(tail_here, "rep", axis=1, tiled=True)
    table_rows = tails.shape[1]
    causal_masks, indices = layout(cont_start, cont_map, continuation_row_block, receptive_width)
    widened_input = jnp.concatenate([halo_rows, prompt_act], axis=1)
    prompt_kernel_taps = jnp.concatenate(
        [
            widened_input[
                :,
                receptive_width
                - kernel_tap_index * DILATION_STEP : receptive_width
                - kernel_tap_index * DILATION_STEP
                + prompt_row_block,
            ]
            for kernel_tap_index in range(3)
        ],
        axis=-1,
    )
    widened_continuation = jnp.concatenate(
        [jnp.zeros((batches, receptive_width, inner), jnp.bfloat16), cont_act], axis=1
    )
    cont_pieces = []
    for kernel_tap_index in range(3):
        nearby_rows = widened_continuation[
            :,
            receptive_width
            - kernel_tap_index * DILATION_STEP : receptive_width
            - kernel_tap_index * DILATION_STEP
            + continuation_row_block,
        ]
        if kernel_tap_index == 0:
            cont_pieces.append(nearby_rows)
        else:
            distant_rows = pick_rows(tails, indices[kernel_tap_index])
            cont_pieces.append(
                jnp.where(causal_masks[kernel_tap_index][..., None], nearby_rows, distant_rows)
            )
    taps = jnp.concatenate([prompt_kernel_taps, jnp.concatenate(cont_pieces, axis=-1)], axis=1)
    conv_flat = low_conv.reshape(3 * inner, inner)
    conv_out = (
        jnp.einsum("mrk,ke->mre", taps, conv_flat, preferred_element_type=jnp.float32) + bias_conv
    )
    pre_three, normed_three, scale_three = norm_forward(conv_out, norm3_gain, norm3_bias)
    act_conv = jax.nn.silu(pre_three).astype(jnp.bfloat16)
    branch_out = (
        jnp.einsum("mri,id->mrd", act_conv, low_out, preferred_element_type=jnp.float32) + bias_out
    )
    block_out = (rows_in + branch_out).astype(jnp.bfloat16)
    back_in, back_conv, back_out = (
        lax.all_gather(w_in.astype(jnp.bfloat16), "shard", axis=0, tiled=True),
        lax.all_gather(w_conv.astype(jnp.bfloat16), "shard", axis=1, tiled=True),
        lax.all_gather(w_out.astype(jnp.bfloat16), "shard", axis=0, tiled=True),
    )
    grad_low = jnp.concatenate([prompt_cot[:, 0], cont_cot[:, 0]], axis=1)
    grad_rows = grad_low.astype(jnp.float32)
    part_bias_out = row_total(grad_rows)
    full_w_out = jnp.einsum("mri,mrd->id", act_conv, grad_low, preferred_element_type=jnp.float32)
    grad_act_conv = jnp.einsum(
        "mrd,id->mri", grad_low, back_out, preferred_element_type=jnp.float32
    )
    grad_act_conv = grad_act_conv * silu_slope(pre_three)
    part_gain_three = row_total(grad_act_conv * normed_three)
    part_shift_three = row_total(grad_act_conv)
    grad_conv_out = norm_backward(grad_act_conv, normed_three, scale_three, norm3_gain)
    part_bias_conv = row_total(grad_conv_out)
    grad_conv_low = grad_conv_out.astype(jnp.bfloat16)
    full_w_conv = jnp.einsum(
        "mrk,mre->ke", taps, grad_conv_low, preferred_element_type=jnp.float32
    ).reshape(3, inner, inner)
    grad_taps = jnp.einsum(
        "mre,ke->mrk",
        grad_conv_low,
        back_conv.reshape(3 * inner, inner),
        preferred_element_type=jnp.float32,
    )
    grad_extended = 0.0
    grad_extended_cont = 0.0
    tail_part = jnp.zeros((batches, table_rows, inner), jnp.float32)
    for kernel_tap_index in range(3):
        prompt_portion = grad_taps[
            :, :prompt_row_block, kernel_tap_index * inner : (kernel_tap_index + 1) * inner
        ]
        grad_extended = grad_extended + jnp.pad(
            prompt_portion,
            (
                (0, 0),
                (
                    receptive_width - kernel_tap_index * DILATION_STEP,
                    kernel_tap_index * DILATION_STEP,
                ),
                (0, 0),
            ),
        )
        cont_piece = grad_taps[
            :, prompt_row_block:, kernel_tap_index * inner : (kernel_tap_index + 1) * inner
        ]
        keep_near = causal_masks[kernel_tap_index][..., None]
        grad_extended_cont = grad_extended_cont + jnp.pad(
            jnp.where(keep_near, cont_piece, 0.0),
            (
                (0, 0),
                (
                    receptive_width - kernel_tap_index * DILATION_STEP,
                    kernel_tap_index * DILATION_STEP,
                ),
                (0, 0),
            ),
        )
        if kernel_tap_index > 0:
            far_piece = jnp.where(keep_near, 0.0, cont_piece)
            tail_part = tail_part + jax.vmap(
                lambda values, where_to: jax.ops.segment_sum(
                    values, where_to, num_segments=table_rows
                )
            )(far_piece, indices[kernel_tap_index])
    back_rim = passed_along(
        grad_extended[:, :receptive_width].astype(jnp.bfloat16), "shard", -1
    ).astype(jnp.float32)
    tail_total, grad_bias_conv, grad_norm3_gain, grad_norm3_bias, grad_bias_out = lax.psum(
        (tail_part, part_bias_conv, part_gain_three, part_shift_three, part_bias_out),
        ("rep", "shard"),
    )
    own_tail = lax.dynamic_slice_in_dim(
        tail_total, lax.axis_index("rep") * receptive_width, receptive_width, 1
    )
    rim_grad = back_rim + jnp.where(lax.axis_index("shard") == last_shard, own_tail, 0.0)
    grad_prompt_act = grad_extended[:, receptive_width:]
    grad_prompt_act = jnp.concatenate(
        [
            grad_prompt_act[:, : prompt_row_block - receptive_width],
            grad_prompt_act[:, prompt_row_block - receptive_width :] + rim_grad,
        ],
        axis=1,
    )
    grad_act_mid = jnp.concatenate(
        [grad_prompt_act, grad_extended_cont[:, receptive_width:]], axis=1
    )
    grad_act_mid = grad_act_mid * silu_slope(pre_two)
    part_gain_two = row_total(grad_act_mid * normed_two)
    part_shift_two = row_total(grad_act_mid)
    grad_hidden = norm_backward(grad_act_mid, normed_two, scale_two, norm2_gain)
    part_bias_in = row_total(grad_hidden)
    grad_hidden_low = grad_hidden.astype(jnp.bfloat16)
    full_w_in = jnp.einsum(
        "mrd,mre->de", act_in, grad_hidden_low, preferred_element_type=jnp.float32
    )
    grad_act_in = jnp.einsum(
        "mre,de->mrd", grad_hidden_low, back_in, preferred_element_type=jnp.float32
    )
    grad_act_in = grad_act_in * silu_slope(pre_one)
    part_gain_one = row_total(grad_act_in * normed_one)
    part_shift_one = row_total(grad_act_in)
    grad_inputs = grad_rows + norm_backward(grad_act_in, normed_one, scale_one, norm1_gain)
    grad_norm1_gain, grad_norm1_bias, grad_bias_in, grad_norm2_gain, grad_norm2_bias = lax.psum(
        (part_gain_one, part_shift_one, part_bias_in, part_gain_two, part_shift_two),
        ("rep", "shard"),
    )
    owned_in, owned_conv, owned_out = (
        lax.psum_scatter(full_w_in, "shard", scatter_dimension=0, tiled=True),
        lax.psum_scatter(full_w_conv, "shard", scatter_dimension=1, tiled=True),
        lax.psum_scatter(full_w_out, "shard", scatter_dimension=0, tiled=True),
    )
    grad_w_in, grad_w_conv, grad_w_out = lax.psum((owned_in, owned_conv, owned_out), "rep")
    prompt_out = block_out[:, None, :prompt_row_block]
    cont_out = block_out[:, None, prompt_row_block:]
    prompt_grad = grad_inputs[:, None, :prompt_row_block]
    cont_grad = grad_inputs[:, None, prompt_row_block:]
    return (
        prompt_out,
        cont_out,
        prompt_grad,
        cont_grad,
        grad_w_in,
        grad_w_conv,
        grad_w_out,
        grad_norm1_gain,
        grad_norm1_bias,
        grad_bias_in,
        grad_norm2_gain,
        grad_norm2_bias,
        grad_bias_conv,
        grad_norm3_gain,
        grad_norm3_bias,
        grad_bias_out,
    )


def solution(mesh):
    in_specs = (
        P(None, "rep", "shard", None),
        P(None, ("rep", "shard"), None, None),
        P(None, ("rep", "shard"), None),
        P(None, ("rep", "shard"), None),
        P("shard", None),
        P(None, "shard", None),
        P("shard", None),
        P(),
        P(),
        P(),
        P(),
        P(),
        P(),
        P(),
        P(),
        P(),
        P(None, "rep", "shard", None),
        P(None, ("rep", "shard"), None, None),
    )
    out_specs = (
        P(None, "rep", "shard", None),
        P(None, ("rep", "shard"), None, None),
        P(None, "rep", "shard", None),
        P(None, ("rep", "shard"), None, None),
        P("shard", None),
        P(None, "shard", None),
        P("shard", None),
        P(),
        P(),
        P(),
        P(),
        P(),
        P(),
        P(),
        P(),
        P(),
    )
    return jax.shard_map(
        on_device, mesh=mesh, in_specs=in_specs, out_specs=out_specs, check_vma=False
    )
```

profile of v0, /device:TPU:0, one launch (start us, length us, event | category | flops | bytes accessed | tf_op | source)
XLA Modules:
  0.0 958.7 jit_solution(8579557248888360181)
XLA Ops:
  7.3 8.4 convert_reduce_fusion
  15.9 4.0 fusion.25
  20.0 21.7 %all_gather.15 = bf16[800,400]{1,0:T(8,128)(2,1)S(1)} all-gather(bf16[200,400]{1,0:T(8,128)(2,1)S(1)} %convert_element_type.56), channel_id=1, replica_groups=mesh['rep'=8,'shard'=4] {'shard'}, dimensions={0}, use_global_device_ids=true | all-gather | bytes 800000 | tf_op jit(solution)/shard_map/all_gather | solution.py:103
  41.7 11.6 %fusion.17 = bf16[8,1024,800]{1,2,0:T(8,128)(2,1)} fusion(f32[800]{0:T(1024)S(1)} %copy-done.37, f32[800]{0:T(1024)S(1)} %copy-done.30, f32[8,1024]{1,0:T(8,128)S(1)} %add_rsqrt_fusion.2, f32[8,1024]{1,0:T(8,128)S(1)} %broadcast_multiply_fusion.8, bf16[8,512,800]{1,2,0:T(8,128)(2,1)S(1)} %bitcast.106, bf16[8,512,800]{1,2,0:T(8,128)(2,1)S(1)} %bitcast.114), kind=kLoop, calls=%fused_computation.27 | loop fusion | flops 85196800 | bytes 26286336 | tf_op jit(solution)/shard_map/convert_element_type | solution.py:109
  53.3 14.4 %add_reduce_fusion.1 = (f32[8,1024]{1,0:T(8,128)S(1)}, f32[8,1024,400]{1,2,0:T(8,128)S(1)}) fusion(f32[400]{0:T(512)S(1)} %copy-done.26, bf16[8,1024,800]{1,2,0:T(8,128)(2,1)} %fusion.17, bf16[800,400]{1,0:T(8,128)(2,1)S(1)} %all_gather.15), kind=kOutput, calls=%fused_computation.66 | convolution fusion | flops 5249425408 | bytes 26888768 | tf_op jit(solution)/shard_map/mrd,de->mre/dot_general | solution.py:111
  67.8 4.9 copy-done
  75.3 8.0 multiply_convert_fusion.1
  91.1 43.4 %all-reduce.17.cloned.1.call-done = bf16[8,32,400]{1,2,0:T(8,128)(2,1)} async-done(((bf16[8,32,400]{1,2,0:T(8,128)(2,1)}), bf16[8,32,400]{1,2,0:T(8,128)(2,1)}) %all-reduce.17.cloned.1.call-update) | async-done | bytes 204816 | tf_op jit(solution)/shard_map/psum | solution.py:20
  138.9 17.7 %all-gather = bf16[4,100,800]{2,1,0:T(8,128)(2,1)S(1)} all-gather(bf16[1,100,800]{2,1,0:T(8,128)(2,1)S(1)} %convert_bitcast_fusion), channel_id=1, replica_groups=mesh['rep'=8,'shard'=4] {'shard'}, dimensions={0}, use_global_device_ids=true | all-gather | bytes 800000 | tf_op jit(solution)/shard_map/all_gather | solution.py:105
  157.8 28.1 %all_gather.17 = bf16[3,400,400]{2,0,1:T(4,128)(2,1)S(1)} all-gather(bf16[3,100,400]{2,0,1:T(4,128)(2,1)S(1)} %copy.125), channel_id=1, replica_groups=mesh['rep'=8,'shard'=4] {'shard'}, dimensions={1}, use_global_device_ids=true | all-gather | bytes 1200000 | tf_op jit(solution)/shard_map/all_gather | solution.py:104
  189.1 5.2 fusion.63
  197.5 4.0 fusion.32
  203.8 47.6 %gather_fusion.1 = bf16[4096,400]{1,0:T(8,128)(2,1)} fusion(bf16[8,256,400]{2,1,0:T(8,128)(2,1)S(1)} %copy.119, s32[4096]{0:T(1024)S(1)} %bitcast.97), kind=kCustom, calls=%fused_computation.1 | custom fusion | bytes 6586368 | tf_op jit(solution)/shard_map/vmap()/gather | solution.py:73
  251.3 6.3 copy.124
  257.6 47.6 %gather_fusion = bf16[4096,400]{1,0:T(8,128)(2,1)} fusion(bf16[8,256,400]{2,1,0:T(8,128)(2,1)S(1)} %copy.119, s32[4096]{0:T(1024)S(1)} %bitcast.96), kind=kCustom, calls=%fused_computation | custom fusion | bytes 6586368 | tf_op jit(solution)/shard_map/vmap()/gather | solution.py:73
  305.2 6.4 copy.121
  311.6 9.7 %fusion.30 = (bf16[8,512,400]{1,2,0:T(8,128)(2,1)}, bf16[8,512,400]{1,2,0:T(8,128)(2,1)}) fusion(bf16[8,512,400]{1,2,0:T(8,128)(2,1)} %copy.121, bf16[8,512,400]{1,2,0:T(8,128)(2,1)} %get-tuple-element.152, pred[8,512]{1,0:T(8,128)(4,1)S(1)} %get-tuple-element.162, bf16[8,512,400]{1,2,0:T(8,128)(2,1)} %copy.124, pred[8,512]{1,0:T(8,128)(4,1)S(1)} %get-tuple-element.161), kind=kLoop, calls=%fused_computation.81 | loop fusion | flops 3276800 | bytes 16392192 | tf_op jit(solution)/shard_map/jit(_where)/select_n | solution.py:154
  321.4 13.6 %fusion.29 = bf16[8,1024,1200]{1,2,0:T(8,128)(2,1)} fusion(bf16[8,512,400]{1,2,0:T(8,128)(2,1)} %copy-done.5, bf16[8,32,400]{1,2,0:T(8,128)(2,1)} %copy.117, bf16[8,512,400]{1,2,0:T(8,128)(2,1)} %get-tuple-element.157, bf16[8,512,400]{1,2,0:T(8,128)(2,1)} %get-tuple-element.156, bf16[8,512,400]{1,2,0:T(8,128)(2,1)S(1)} %copy-done.4, ...), kind=kLoop, calls=%fused_computation.40 | loop fusion | flops 186777600 | bytes 36249600 | tf_op jit(solution)/shard_map/concatenate | solution.py:156
  335.0 15.7 %add_reduce_fusion = (f32[8,1024]{1,0:T(8,128)S(1)}, f32[8,1024,400]{1,2,0:T(8,128)S(1)}) fusion(f32[400]{0:T(512)S(1)} %copy-done.36, bf16[8,1024,1200]{1,2,0:T(8,128)(2,1)} %fusion.29, bf16[1200,400,1]{1,0,2:T(8,128)(2,1)} %bitcast.132), kind=kOutput, calls=%fused_computation.65 | convolution fusion | flops 7870865408 | bytes 33762368 | tf_op jit(solution)/shard_map/mrk,ke->mre/dot_general | solution.py:159
  352.7 18.3 %multiply_reduce_fusion.1 = (f32[400]{0:T(512)}, f32[8,1024]{1,0:T(8,128)S(1)}, f32[8,1024]{1,0:T(8,128)S(1)}, f32[400]{0:T(512)}, f32[8,1024,400]{1,2,0:T(8,128)}) fusion(f32[8,1024]{1,0:T(8,128)S(1)} %add_rsqrt_fusion, f32[8,1024]{1,0:T(8,128)S(1)} %broadcast_multiply_fusion.4, f32[8,1024,400]{1,2,0:T(8,128)S(1)} %get-tuple-element.168, ...), kind=kOutput, calls=%fused_computation.46 | convolution fusion | flops 5334612992 | bytes 40100672 | tf_op jit(solution)/shard_map/mrd,id->mri/dot_general | solution.py:176
  371.1 13.8 %fusion.61 = (f32[400]{0:T(512)}, bf16[8,1024,400]{1,2,0:T(8,128)(2,1)}, bf16[8,1024,400]{1,2,0:T(8,128)(2,1)}) fusion(f32[8,1024]{1,0:T(8,128)S(1)} %get-tuple-element.171, f32[8,1024]{1,0:T(8,128)S(1)} %broadcast_multiply_fusion.4, f32[8,1024,400]{1,2,0:T(8,128)S(1)} %get-tuple-element.168, f32[400]{0:T(512)S(1)} %copy-done.36, ...), kind=kLoop, calls=%fused_computation.150 | loop fusion | flops 55705200 | bytes 39459072 | tf_op jit(solution)/shard_map/reduce_sum | solution.py:45
  384.9 20.0 %fusion.36 = f32[1200,400,1]{1,0,2:T(8,128)} fusion(bf16[8,1024,1200]{1,2,0:T(8,128)(2,1)} %fusion.29, bf16[8,1024,400]{1,2,0:T(8,128)(2,1)} %get-tuple-element.127), kind=kOutput, calls=%fused_computation.87 | convolution fusion | flops 7864320000 | bytes 28134400 | tf_op jit(solution)/shard_map/mrk,mre->ke/dot_general | solution.py:185
  404.9 16.9 %fusion.38 = f32[8,1024,1200]{1,2,0:T(8,128)} fusion(bf16[1200,400,1]{1,0,2:T(8,128)(2,1)S(1)} %bitcast.133, bf16[8,1024,400]{1,2,0:T(8,128)(2,1)S(1)} %copy-done.6), kind=kOutput, calls=%fused_computation.89 | convolution fusion | flops 7864320000 | bytes 46835200 | tf_op jit(solution)/shard_map/mre,ke->mrk/dot_general | solution.py:188
  421.9 13.6 %convolution_bitcast_fusion = f32[400,800]{1,0:T(8,128)S(1)} fusion(bf16[8,1024,400]{1,2,0:T(8,128)(2,1)} %get-tuple-element.147, bf16[8,512,800]{1,2,0:T(8,128)(2,1)} %bitcast.126, bf16[8,512,800]{1,2,0:T(8,128)(2,1)} %bitcast.129), kind=kOutput, calls=%fused_computation.98 | convolution fusion | flops 5269094400 | bytes 20940800 | tf_op jit(solution)/shard_map/mri,mrd->id/dot_general | solution.py:175
  435.5 30.3 %fusion = f32[112,800]{1,0:T(8,128)S(1)} fusion(f32[400,800]{1,0:T(8,128)S(1)} %convolution_bitcast_fusion), kind=kCustom, calls=%all-reduce-scatter | all-reduce-scatter fusion | flops 358401 | bytes 1638912
  467.9 16.2 %fusion.26 = bf16[8,1024,800]{1,2,0:T(8,128)(2,1)} fusion(f32[800]{0:T(1024)S(1)} %copy-done.48, bf16[8,1024,400]{1,2,0:T(8,128)(2,1)} %get-tuple-element.147, bf16[400,800,1]{1,0,2:T(8,128)(2,1)S(1)} %copy-done.12, bf16[8,512,800]{1,2,0:T(8,128)(2,1)} %bitcast.101, bf16[8,512,800]{1,2,0:T(8,128)(2,1)} %bitcast.111), kind=kOutput, calls=%fused_computation.36 | convolution fusion | flops 5288755200 | bytes 33411200 | tf_op jit(solution)/shard_map/mri,id->mrd/dot_general | solution.py:164
  484.1 30.9 %slice_select_fusion.2 = (f32[8,512,400]{1,2,0:T(8,128)}, f32[8,512,400]{1,2,0:T(8,128)}, f32[8,512,400]{1,2,0:T(8,128)}, f32[8,512,400]{1,2,0:T(8,128)}, f32[8,...) fusion(f32[8,1024,1200]{1,2,0:T(8,128)} %fusion.38, ...), kind=kLoop, calls=%fused_computation.74 | loop fusion | flops 8192000 | bytes 91762688 | tf_op jit(solution)/shard_map/jit(_where)/select_n | solution.py:228
  515.0 8.5 copy.155
  523.5 8.5 copy.154
  532.0 31.4 %scatter_custom_fusion.1 = f32[2048,400]{1,0:T(8,128)} fusion(s32[4096]{0:T(1024)} %bitcast.135, f32[4096,400]{1,0:T(8,128)} %bitcast.124, f32[]{:T(128)} %constant.48.clone.1), kind=kCustom, calls=%fused_computation.91 | custom fusion | flops 1638400 | bytes 3277312
  563.4 31.7 %scatter_custom_fusion = f32[2048,400]{1,0:T(8,128)} fusion(s32[4096]{0:T(1024)} %bitcast.134, f32[4096,400]{1,0:T(8,128)} %bitcast.123, f32[]{:T(128)} %constant.48.clone.1), kind=kCustom, calls=%fused_computation.93 | custom fusion | flops 1638400 | bytes 3277312
  595.0 6.5 add.295
  601.5 5.2 copy.136
  606.8 9.3 pad_add_fusion
  616.2 3.1 copy-done.2
  621.1 10.7 %slice_bitcast_fusion.2 = (bf16[8,1,512,800]{2,3,1,0:T(8,128)(2,1)}, bf16[8,1,512,800]{2,3,1,0:T(8,128)(2,1)}) fusion(bf16[8,1024,800]{1,2,0:T(8,128)(2,1)} %fusion.26), kind=kLoop, calls=%fused_computation.71 | loop fusion | bytes 26214400
  631.8 11.0 %pad_add_fusion.1 = f32[8,512,400]{1,2,0:T(8,128)} fusion(f32[8,512,400]{1,2,0:T(8,128)} %get-tuple-element.136, f32[8,512,400]{1,2,0:T(8,128)} %get-tuple-element.140, f32[8,512,400]{1,2,0:T(8,128)} %get-tuple-element.139), kind=kLoop, calls=%fused_computation.68 | loop fusion | flops 3276800 | bytes 26214400 | tf_op jit(solution)/shard_map/add | solution.py:216
  642.9 8.1 slice.103
  652.5 92.6 %all-reduce.19.cloned.1.call-done = f32[8,256,400]{1,2,0:T(8,128)} async-done(((f32[8,256,400]{1,2,0:T(8,128)}), f32[8,256,400]{1,2,0:T(8,128)}) %all-reduce.19.cloned.1.call-update) | async-done | bytes 3276816 | tf_op jit(solution)/shard_map/psum | solution.py:237
  747.7 21.0 %multiply_reduce_fusion.2 = (f32[400]{0:T(512)S(1)}, f32[8,1024]{1,0:T(8,128)S(1)}, f32[8,1024]{1,0:T(8,128)S(1)}, f32[400]{0:T(512)S(1)}, f32[8,1024,400]{1,2,0:T(8,128)}) fusion(f32[8,1024]{1,0:T(8,128)S(1)} %copy-done.17, f32[8,1024]{1,0:T(8,128)S(1)} %copy-done.10, f32[8,1024,400]{1,2,0:T(8,128)} %copy-done, f32[400]{0:T(512)S(1)} %copy-done.27, ...), kind=kLoop, calls=%fused_computation.47 | loop fusion | flops 72072416 | bytes 39460672 | tf_op jit(solution)/shard_map/reduce_sum | solution.py:45
  768.8 10.1 %fusion.62 = (f32[400]{0:T(512)S(1)}, bf16[8,1024,400]{1,2,0:T(8,128)(2,1)}) fusion(f32[8,1024]{1,0:T(8,128)S(1)} %broadcast_multiply_fusion, f32[8,1024]{1,0:T(8,128)S(1)} %copy-done.10, f32[8,1024,400]{1,2,0:T(8,128)S(1)} %bitcast.99, f32[400]{0:T(512)S(1)} %copy-done.27, f32[8,1024]{1,0:T(8,128)S(1)} %broadcast_multiply_fusion.1, ...), kind=kLoop, calls=%fused_computation.151 | loop fusion | flops 32767600 | bytes 32903872 | tf_op jit(solution)/shard_map/reduce_sum | solution.py:45
  779.0 26.0 %fusion.24 = (f32[800]{0:T(1024)S(1)}, f32[8,1024]{1,0:T(8,128)S(1)}, f32[8,1024]{1,0:T(8,128)S(1)}, f32[800]{0:T(1024)S(1)}, f32[8,1024,800]{1,2,0:T(8,128)}) fusion(f32[8,1024]{1,0:T(8,128)S(1)} %copy-done.21, f32[8,1024]{1,0:T(8,128)S(1)} %copy-done.15, bf16[8,512,800]{1,2,0:T(8,128)(2,1)S(1)} %bitcast.109, bf16[8,512,800]{1,2,0:T(8,128)(2,1)S(1)} %bitcast.117, ...), kind=kOutput, calls=%fused_computation.34 | convolution fusion | flops 5393594368 | bytes 46659072 | tf_op jit(solution)/shard_map/mre,de->mrd/dot_general | solution.py:265
  805.1 10.3 %fusion.44 = f32[800,400]{1,0:T(8,128)} fusion(bf16[8,1024,800]{1,2,0:T(8,128)(2,1)S(1)} %bitcast.122, bf16[8,1024,400]{1,2,0:T(8,128)(2,1)} %get-tuple-element.129), kind=kOutput, calls=%fused_computation.97 | convolution fusion | flops 5242880000 | bytes 20940800 | tf_op jit(solution)/shard_map/mrd,mre->de/dot_general | solution.py:262
  815.4 28.3 %convert_reduce_fusion.1 = (f32[800]{0:T(1024)S(1)}, f32[8,1024,800]{1,2,0:T(8,128)}) fusion(bf16[8,512,800]{1,2,0:T(8,128)(2,1)} %bitcast.127, bf16[8,512,800]{1,2,0:T(8,128)(2,1)} %bitcast.130, f32[8,1024]{1,0:T(8,128)S(1)} %broadcast_multiply_fusion.6, f32[8,1024]{1,0:T(8,128)S(1)} %copy-done.15, bf16[8,512,800]{1,2,0:T(8,128)(2,1)} %bitcast.102, ...), kind=kLoop, calls=%fused_computation.12 | loop fusion | flops 111410400 | bytes 78780672 | tf_op jit(solution)/shard_map/reduce_sum | solution.py:45
  847.6 36.2 %reduce-scatter.5.cloned.1.call-done = f32[200,400]{1,0:T(8,128)} async-done(((f32[800,400]{1,0:T(8,128)}), f32[200,400]{1,0:T(8,128)}) %reduce-scatter.5.cloned.1.call-update) | async-done | bytes 320016 | tf_op jit(solution)/shard_map/reduce_scatter | solution.py:277
  883.9 17.0 %slice_bitcast_fusion = (f32[8,1,512,800]{2,3,1,0:T(8,128)}, f32[8,1,512,800]{2,3,1,0:T(8,128)}) fusion(f32[8,1024,800]{1,2,0:T(8,128)} %get-tuple-element.149), kind=kLoop, calls=%fused_computation.41 | loop fusion | bytes 52428800
  901.0 39.9 %all-reduce.10 = (f32[800]{0:T(1024)}, f32[800]{0:T(1024)}, f32[400]{0:T(512)}, f32[400]{0:T(512)}, f32[400]{0:T(512)}, /*index=5*/f32[400]{0:T(512)}, f32[400]{0:T(512)}, f32[400]{0:T(512)}, f32[800]{0:T(1024)}) all-reduce(f32[800]{0:T(1024)S(1)} %get-tuple-element.96, ...), channel_id=1, replica_groups=mesh['rep'=8,'shard'=4] {'rep','shard'}, use_global_device_ids=true, to_apply=%region_26.27 | all-reduce | flops 4800 | bytes 38400 | tf_op jit(solution)/shard_map/psum | solution.py:272
  940.9 4.8 all-reduce.23.cloned.1.call-done
  (198 shorter events, 43.3 us)
Async XLA Ops:
  7.2 127.3 %all-reduce.17.cloned.1.call-start = ((), (), s32[]{:S(2)}) async-start(), calls=%async_computation.1 | async-start | bytes 1638400 | tf_op jit(solution)/shard_map/psum | solution.py:20
  7.3 34.4 %copy-start.30 = (f32[800]{0:T(1024)S(1)}, f32[800]{0:T(1024)}, u32[]{:S(2)}) copy-start(f32[800]{0:T(1024)} %param.25) | copy-start | bytes 9604
  7.3 34.3 %copy-start.37 = (f32[800]{0:T(1024)S(1)}, f32[800]{0:T(1024)}, u32[]{:S(2)}) copy-start(f32[800]{0:T(1024)} %param.26) | copy-start | bytes 9604
  15.9 25.7 %copy-start.14 = (f32[8,1024]{1,0:T(8,128)}, f32[8,1024]{1,0:T(8,128)S(1)}, u32[]{:S(2)}) copy-start(f32[8,1024]{1,0:T(8,128)S(1)} %broadcast_multiply_fusion.8) | copy-start | bytes 98308
  19.9 21.7 %copy-start.20 = (f32[8,1024]{1,0:T(8,128)}, f32[8,1024]{1,0:T(8,128)S(1)}, u32[]{:S(2)}) copy-start(f32[8,1024]{1,0:T(8,128)S(1)} %add_rsqrt_fusion.2) | copy-start | bytes 98308
  74.6 62.2 %copy-start.39 = (s32[8,1,2]{0,2,1:T(2,128)S(1)}, s32[8,1,2]{0,2,1:T(2,128)}, u32[]{:S(2)}) copy-start(s32[8,1,2]{0,2,1:T(2,128)} %param.21) | copy-start | bytes 196
  74.7 62.3 %copy-start.45 = (s32[8,1,2]{0,2,1:T(2,128)S(1)}, s32[8,1,2]{0,2,1:T(2,128)}, u32[]{:S(2)}) copy-start(s32[8,1,2]{0,2,1:T(2,128)} %param.20) | copy-start | bytes 196
  74.7 62.4 %copy-start.47 = (s32[2]{0:T(128)S(1)}, s32[2]{0:T(128)}, u32[]{:S(2)}) copy-start(s32[2]{0:T(128)} %constant.84) | copy-start | bytes 28
  74.7 62.5 %copy-start.46 = (s32[2]{0:T(128)S(1)}, s32[2]{0:T(128)}, u32[]{:S(2)}) copy-start(s32[2]{0:T(128)} %constant.87) | copy-start | bytes 28
  74.7 63.8 %copy-start.13 = (f32[3,100,400]{1,2,0:T(8,128)S(1)}, f32[3,100,400]{1,2,0:T(8,128)}, u32[]{:S(2)}) copy-start(f32[3,100,400]{1,2,0:T(8,128)} %param.23) | copy-start | bytes 1440004
  75.3 63.6 %copy-start.19 = (f32[100,800]{1,0:T(8,128)S(1)}, f32[100,800]{1,0:T(8,128)}, u32[]{:S(2)}) copy-start(f32[100,800]{1,0:T(8,128)} %param.24) | copy-start | bytes 960004
  75.3 111.9 %copy-start.44 = (u32[32]{0:T(128)S(1)}, u32[32]{0:T(128)}, u32[]{:S(2)}) copy-start(u32[32]{0:T(128)} %constant.127) | copy-start | bytes 388
  87.4 114.1 %all-gather.3.cloned.1.call-start = ((), (), s32[]{:S(2)}) async-start(), calls=%async_computation.2 | async-start | bytes 2359296 | tf_op jit(solution)/shard_map/all_gather | solution.py:120
  88.8 106.2 %collective-permute-start = (bf16[8,32,400]{2,1,0:T(8,128)(2,1)}, bf16[8,32,400]{2,1,0:T(8,128)(2,1)}, u32[]{:S(2)}, u32[]{:S(2)}) collective-permute-start(bf16[8,32,400]{2,1,0:T(8,128)(2,1)} %copy.116), channel_id=1, source_target_pairs={{0,1},{1,2},{2,3},{4,5},{5,6},{6,7},{8,9},{9,10},{10,11},{12,13},{... | collective-permute-start | bytes 614408 | tf_op jit(solution)/shard_map/ppermute | solution.py:15
  136.8 608.2 %all-reduce.19.cloned.1.call-start = ((), (), s32[]{:S(2)}) async-start(), calls=%async_computation.3 | async-start | bytes 6553600 | tf_op jit(solution)/shard_map/psum | solution.py:237
  195.0 116.6 %copy-start.22 = (pred[8,512]{1,0:T(8,128)(4,1)}, pred[8,512]{1,0:T(8,128)(4,1)S(1)}, u32[]{:S(2)}) copy-start(pred[8,512]{1,0:T(8,128)(4,1)S(1)} %get-tuple-element.161) | copy-start | bytes 12292
  195.0 116.6 %copy-start.24 = (pred[8,512]{1,0:T(8,128)(4,1)}, pred[8,512]{1,0:T(8,128)(4,1)S(1)}, u32[]{:S(2)}) copy-start(pred[8,512]{1,0:T(8,128)(4,1)S(1)} %get-tuple-element.162) | copy-start | bytes 12292
  384.9 20.0 %copy-start.6 = (bf16[8,1024,400]{1,2,0:T(8,128)(2,1)S(1)}, bf16[8,1024,400]{1,2,0:T(8,128)(2,1)}, u32[]{:S(2)}) copy-start(bf16[8,1024,400]{1,2,0:T(8,128)(2,1)} %get-tuple-element.127) | copy-start | bytes 19660804
  384.9 20.0 %copy-start.7 = (bf16[3,400,400]{2,1,0:T(8,128)(2,1)S(1)}, bf16[3,400,400]{2,1,0:T(8,128)(2,1)}, u32[]{:S(2)}) copy-start(bf16[3,400,400]{2,1,0:T(8,128)(2,1)} %copy.126) | copy-start | bytes 2880004
  421.9 46.1 %copy-start.12 = (bf16[400,800,1]{1,0,2:T(8,128)(2,1)S(1)}, bf16[400,800,1]{1,0,2:T(8,128)(2,1)}, u32[]{:S(2)}) copy-start(bf16[400,800,1]{1,0,2:T(8,128)(2,1)} %reshape.260) | copy-start | bytes 1920004
  421.9 46.1 %copy-start.48 = (f32[800]{0:T(1024)S(1)}, f32[800]{0:T(1024)}, u32[]{:S(2)}) copy-start(f32[800]{0:T(1024)} %param.33) | copy-start | bytes 9604
  465.8 18.3 %copy-start.23 = (pred[8,512]{1,0:T(8,128)(4,1)S(1)}, pred[8,512]{1,0:T(8,128)(4,1)}, u32[]{:S(2)}) copy-start(pred[8,512]{1,0:T(8,128)(4,1)} %copy-done.22) | copy-start | bytes 12292
  465.8 18.3 %copy-start.25 = (pred[8,512]{1,0:T(8,128)(4,1)S(1)}, pred[8,512]{1,0:T(8,128)(4,1)}, u32[]{:S(2)}) copy-start(pred[8,512]{1,0:T(8,128)(4,1)} %copy-done.24) | copy-start | bytes 12292
  465.8 18.3 %copy-start.32 = (pred[8,512]{1,0:T(8,128)(4,1)S(1)}, pred[8,512]{1,0:T(8,128)(4,1)}, u32[]{:S(2)}) copy-start(pred[8,512]{1,0:T(8,128)(4,1)} %get-tuple-element.160) | copy-start | bytes 12292
  465.8 185.1 %collective-permute-start.2 = (f32[36,800]{1,0:T(8,128)S(1)}, f32[36,800]{1,0:T(8,128)S(1)}, u32[]{:S(2)}, u32[]{:S(2)}) collective-permute-start(f32[36,800]{1,0:T(8,128)S(1)} %slice.111), channel_id=1, source_target_pairs={{0,1},{1,2},{2,3},{4,5},{5,6},{6,7},{8,9},{9,10},{10,11},{12,13},{... | collective-permute-start | bytes 345608
  606.8 238.8 %all-reduce.21.cloned.1.call-start = ((), (), s32[]{:S(2)}) async-start(), calls=%async_computation.5 | async-start | bytes 4915200
  619.8 32.3 %collective-permute-start.1 = (bf16[8,32,400]{2,1,0:T(8,128)(2,1)S(1)}, bf16[8,32,400]{2,1,0:T(8,128)(2,1)S(1)}, u32[]{:S(2)}, u32[]{:S(2)}) collective-permute-start(bf16[8,32,400]{2,1,0:T(8,128)(2,1)S(1)} %copy.129), channel_id=1, source_target_pairs={{1,0},{2,1},{3,2},{5,4},{6,5},{7,6},{9,8},{10,9},{11,10},{13,12},{... | collective-permute-start | bytes 614408 | tf_op jit(solution)/shard_map/ppermute | solution.py:15
  631.8 252.0 %reduce-scatter.5.cloned.1.call-start = ((), (), s32[]{:S(2)}) async-start(), calls=%async_computation.4 | async-start | bytes 2048000 | tf_op jit(solution)/shard_map/reduce_scatter | solution.py:277
  642.8 104.8 %copy-start.10 = (f32[8,1024]{1,0:T(8,128)S(1)}, f32[8,1024]{1,0:T(8,128)}, u32[]{:S(2)}) copy-start(f32[8,1024]{1,0:T(8,128)} %copy-done.9) | copy-start | bytes 98308
  642.8 104.8 %copy-start.17 = (f32[8,1024]{1,0:T(8,128)S(1)}, f32[8,1024]{1,0:T(8,128)}, u32[]{:S(2)}) copy-start(f32[8,1024]{1,0:T(8,128)} %copy-done.16) | copy-start | bytes 98308
  642.8 104.8 %copy-start.27 = (f32[400]{0:T(512)S(1)}, f32[400]{0:T(512)}, u32[]{:S(2)}) copy-start(f32[400]{0:T(512)} %param.27) | copy-start | bytes 4804
  642.8 104.8 %copy-start.29 = (f32[400]{0:T(512)S(1)}, f32[400]{0:T(512)}, u32[]{:S(2)}) copy-start(f32[400]{0:T(512)} %param.28) | copy-start | bytes 4804
  642.9 104.8 %copy-start.34 = (f32[400]{0:T(512)S(1)}, f32[400]{0:T(512)}, u32[]{:S(2)}) copy-start(f32[400]{0:T(512)} %param.29) | copy-start | bytes 4804
  745.0 23.7 %slice-start = ((s8[13107200]{0:T(1024)(128)(4,1)}), s8[4194304]{0:T(1024)(128)(4,1)S(1)}, s32[]{:S(2)}) async-start(s8[13107200]{0:T(1024)(128)(4,1)} %bitcast.98), calls=%async_computation.7 | async-start | bytes 8388608
  745.0 33.9 %slice-start.6 = ((s8[6553600]{0:T(1024)(128)(4,1)}), s8[4194304]{0:T(1024)(128)(4,1)S(1)}, s32[]{:S(2)}) async-start(s8[6553600]{0:T(1024)(128)(4,1)} %bitcast.107), calls=%async_computation.13 | async-start | bytes 8388608
  745.0 33.9 %slice-start.8 = ((s8[6553600]{0:T(1024)(128)(4,1)}), s8[4194304]{0:T(1024)(128)(4,1)S(1)}, s32[]{:S(2)}) async-start(s8[6553600]{0:T(1024)(128)(4,1)} %bitcast.115), calls=%async_computation.15 | async-start | bytes 8388608
  747.7 21.1 %slice-start.1 = ((s8[13107200]{0:T(1024)(128)(4,1)}), s8[4194304]{0:T(1024)(128)(4,1)S(1)}, s32[]{:S(2)}) async-start(s8[13107200]{0:T(1024)(128)(4,1)} %bitcast.98), calls=%async_computation.8 | async-start | bytes 8388608
  747.7 21.1 %slice-start.2 = ((s8[13107200]{0:T(1024)(128)(4,1)}), s8[4194304]{0:T(1024)(128)(4,1)S(1)}, s32[]{:S(2)}) async-start(s8[13107200]{0:T(1024)(128)(4,1)} %bitcast.98), calls=%async_computation.9 | async-start | bytes 8388608
  747.7 21.1 %slice-start.3 = ((s8[13107200]{0:T(1024)(128)(4,1)}), s8[524288]{0:T(1024)(128)(4,1)S(1)}, s32[]{:S(2)}) async-start(s8[13107200]{0:T(1024)(128)(4,1)} %bitcast.98), calls=%async_computation.10 | async-start | bytes 1048576
  747.7 31.2 %slice-start.7 = ((s8[6553600]{0:T(1024)(128)(4,1)}), s8[2359296]{0:T(1024)(128)(4,1)S(1)}, s32[]{:S(2)}) async-start(s8[6553600]{0:T(1024)(128)(4,1)} %bitcast.107), calls=%async_computation.14 | async-start | bytes 4718592
  747.7 31.2 %slice-start.9 = ((s8[6553600]{0:T(1024)(128)(4,1)}), s8[2359296]{0:T(1024)(128)(4,1)S(1)}, s32[]{:S(2)}) async-start(s8[6553600]{0:T(1024)(128)(4,1)} %bitcast.115), calls=%async_computation.16 | async-start | bytes 4718592
  768.8 36.2 %slice-start.10 = ((s8[13107200]{0:T(1024)(128)(4,1)}), s8[524288]{0:T(1024)(128)(4,1)S(1)}, s32[]{:S(2)}) async-start(s8[13107200]{0:T(1024)(128)(4,1)} %bitcast.121), calls=%async_computation.17 | async-start | bytes 1048576
  779.0 26.0 %slice-start.11 = ((s8[13107200]{0:T(1024)(128)(4,1)}), s8[4194304]{0:T(1024)(128)(4,1)S(1)}, s32[]{:S(2)}) async-start(s8[13107200]{0:T(1024)(128)(4,1)} %bitcast.121), calls=%async_computation.18 | async-start | bytes 8388608
  779.0 26.0 %slice-start.12 = ((s8[13107200]{0:T(1024)(128)(4,1)}), s8[4194304]{0:T(1024)(128)(4,1)S(1)}, s32[]{:S(2)}) async-start(s8[13107200]{0:T(1024)(128)(4,1)} %bitcast.121), calls=%async_computation.19 | async-start | bytes 8388608
  779.0 26.0 %slice-start.13 = ((s8[13107200]{0:T(1024)(128)(4,1)}), s8[4194304]{0:T(1024)(128)(4,1)S(1)}, s32[]{:S(2)}) async-start(s8[13107200]{0:T(1024)(128)(4,1)} %bitcast.121), calls=%async_computation.20 | async-start | bytes 8388608
  815.4 130.4 %all-reduce.23.cloned.1.call-start = ((), (), s32[]{:S(2)}) async-start(), calls=%async_computation.6 | async-start | bytes 2842624 | tf_op jit(solution)/shard_map/psum | solution.py:281
  883.9 17.1 %copy-start.35 = (f32[400]{0:T(512)S(1)}, f32[400]{0:T(512)}, u32[]{:S(2)}) copy-start(f32[400]{0:T(512)} %get-tuple-element.126) | copy-start | bytes 4804
  883.9 17.1 %copy-start.42 = (f32[400]{0:T(512)S(1)}, f32[400]{0:T(512)}, u32[]{:S(2)}) copy-start(f32[400]{0:T(512)} %get-tuple-element.98) | copy-start | bytes 4804
  (24 other events, 196.1 us)
Sparse Core Ops, SparseCore 0:
  87.5 46.8 all-reduce.16
  136.9 27.0 all-gather.2
  606.9 138.0 all-reduce.18
  747.4 98.1 all-reduce.20
  848.4 35.3 reduce-scatter.4
  887.8 57.8 all-reduce.22
where the time goes:
time: 968 us; the launch traced here: 959 us
  other arithmetic  262 us (27%)
  local copies, waits for them, and re-layouts  205 us (21%)
  waiting for transfers between devices  179 us (18%)
  matrix products  151 us (16%)
  blocking collectives  138 us (14%)
  between operations  16.9 us (2%)
    gather x4, local copies, waits for them, and re-layouts, pick_rows(): block[where_from]  108 us
    psum x1, waiting for transfers between devices, on_device(): lax.psum((tail_part, part_bias_conv, part_gain_three, part_shift_three, p...  92.6 us
    reduce_sum x4, other arithmetic, row_total(): return jnp.sum(values, axis=(0, 1))  73.2 us
    unnamed x12, other arithmetic  63.2 us
    unnamed x142, local copies, waits for them, and re-layouts  51.5 us
    psum x1, waiting for transfers between devices, from_root(): return lax.psum(kept, axis)  43.4 us
    psum x1, blocking collectives, on_device(): lax.psum((part_gain_one, part_shift_one, part_bias_in, part_gain_two, par...  39.9 us
    reduce_scatter x1, waiting for transfers between devices, on_device(): lax.psum_scatter(full_w_in, 'shard', scatter_dimension=0, tiled=True)  36.2 us
  transfers between devices with their start and end apart: 9, of which 5 were waited for; matrix products, arithmetic and copies ran while one was open for 33% of the time, Pallas kernels for 0%

commit v1 on v0

v1 whole, which is shorter than its diff:
```python
import functools

import jax
import jax.numpy as jnp
from jax import lax
from jax.experimental import pallas as pl
from jax.experimental.pallas import tpu as pltpu
from jax.sharding import PartitionSpec as P

STEP = 16
REACH = 2 * STEP
LANES = 128
GROUP = 4
epsilon = 1e-05
bf16 = jnp.bfloat16
f32 = jnp.float32
VMEM_BYTES = 58 * 2**20
WHOLE = pl.BlockSpec(memory_space=pltpu.VMEM)
PARAMS = pltpu.CompilerParams(vmem_limit_bytes=VMEM_BYTES)


def cost(flops, moved):
    return pl.CostEstimate(flops=int(2.5 * flops), bytes_accessed=int(moved), transcendentals=0)


def dot(a, b, ca, cb):
    return lax.dot_general(a, b, (((ca,), (cb,)), ((), ())), preferred_element_type=f32)


def at(column):
    return slice(column * LANES, (column + 1) * LANES)


def where_is(shape, column):
    per = shape[-1] // LANES
    return column // per, at(column % per)


def column_of(ref, column):
    block, lanes = where_is(ref.shape, column)
    return ref[(block,) + (0,) * (len(ref.shape) - 3) + (slice(None), lanes)]


def put_column(ref, column, values):
    block, lanes = where_is(ref.shape, column)
    ref[(block,) + (0,) * (len(ref.shape) - 3) + (slice(None), lanes)] = values


def columns_in(ref):
    return ref.shape[0] * (ref.shape[-1] // LANES)


def mean_over(values):
    return jnp.sum(values, axis=0, keepdims=True) * (1.0 / values.shape[0])


def normed_of(x):
    center = x - mean_over(x)
    scale = lax.rsqrt(mean_over(center * center) + epsilon)
    return center * scale, scale


def silu(y):
    half = 0.5 * y
    return half * jnp.tanh(half) + half


def silu_and_slope(y):
    half = 0.5 * y
    t = jnp.tanh(half)
    value = half * t + half
    sigma = 0.5 * t + 0.5
    return value, sigma + value * (1.0 - sigma)


def norm_backward(g, normed, scale, gain):
    gn = g * normed
    u = g * gain
    return gn, scale * (u - mean_over(u) - normed * mean_over(gn * gain))


def front_kernel(streams, with_rim, *refs):
    x_refs, refs = refs[:streams], refs[streams:]
    (w_in_t, vec1, vec2), refs = refs[:3], refs[3:]
    outs, refs = [refs[3 * s : 3 * s + 3] for s in range(streams)], refs[3 * streams :]
    rim_ref = refs[0] if with_rim else None
    acts = refs[-streams:]
    width = vec1.shape[1]
    for s in range(streams):
        x_ref, act = x_refs[s], acts[s]
        mid_ref, n2_ref, r2_ref = outs[s]
        columns = columns_in(x_ref)
        for c in range(columns):
            normed, _ = normed_of(column_of(x_ref, c).astype(f32))
            act[:, at(c)] = silu(normed * vec1[0] + vec1[1]).astype(bf16)
        hidden = dot(w_in_t[...], act[...], 1, 0)
        rim = []
        for c in range(columns):
            normed, scale = normed_of(hidden[:, at(c)] + vec2[0])
            value = silu(normed * vec2[1] + vec2[2])
            put_column(mid_ref, c, value.astype(bf16))
            put_column(n2_ref, c, normed.astype(bf16))
            put_column(r2_ref, c, scale)
            rim.append(value[:, LANES - REACH :])
        if with_rim:
            rim_ref[...] = jnp.concatenate(rim, axis=1).astype(bf16)


def blocks(shape, lanes, group, first):
    full = (group,) + tuple(shape[1:-1]) + (lanes,)
    return pl.BlockSpec(full, lambda i: (i,) + (0,) * (len(shape) - 2) + (first // lanes,))


def front(xs, parts, w_in_t, vec1, vec2, with_rim=False):
    inner, width = w_in_t.shape
    batches = xs[0].shape[0]
    steps = batches // parts[0][1]
    in_specs, out_specs, out_shape, scratch = [], [], [], []
    for x, (lanes, group, first) in zip(xs, parts):
        in_specs.append(blocks(x.shape, lanes, group, first))
        for depth, kind in ((inner, bf16), (inner, bf16), (1, f32)):
            out_specs.append(blocks((batches, depth, lanes), lanes, group, 0))
            out_shape.append(jax.ShapeDtypeStruct((batches, depth, lanes), kind))
        scratch.append(pltpu.VMEM((width, group * lanes), bf16))
    if with_rim:
        out_specs.append(pl.BlockSpec((inner, GROUP * REACH), lambda i: (0, i)))
        out_shape.append(jax.ShapeDtypeStruct((inner, batches * REACH), bf16))
    return pl.pallas_call(
        functools.partial(front_kernel, len(xs), with_rim),
        grid=(steps,),
        in_specs=in_specs + [WHOLE] * 3,
        out_specs=out_specs,
        out_shape=out_shape,
        scratch_shapes=scratch,
        compiler_params=PARAMS,
        cost_estimate=cost(4 * width * inner * sum(batches * part[0] for part in parts), 0),
        name="front",
    )(*xs, w_in_t, vec1, vec2)


def shifted_right(values, by):
    zeros = jnp.zeros((values.shape[0], by), values.dtype)
    return jnp.concatenate([zeros, values[:, : values.shape[1] - by]], axis=1)


def shifted_left(values, by):
    zeros = jnp.zeros((values.shape[0], by), values.dtype)
    return jnp.concatenate([values[:, by:], zeros], axis=1)


def chosen(base, position, fits, batches):
    one = jnp.where(jnp.logical_and(fits, position < STEP), base + STEP + position, -1)
    two = jnp.where(jnp.logical_and(fits, position < REACH), base + position, -1)
    target = jnp.concatenate([one, two], axis=1)
    row = lax.broadcasted_iota(jnp.int32, (batches * REACH, target.shape[1]), 0)
    return jnp.where(row == target, 1.0, 0.0).astype(bf16)


def middle_kernel(batches, prompts, group, pieces, has_before, has_after, *refs):
    if not prompts:
        (cont_start, cont_map), refs = refs[:2], refs[2:]
    mids, refs = refs[:pieces], refs[pieces:]
    (x_ref, cot_ref, tails), refs = refs[:3], refs[3:]
    (w_conv_t, w_conv, w_out_t, w_out, vec3, bias_out), refs = refs[:6], refs[6:]
    if has_before:
        before, refs = refs[:4], refs[4:]
    out_ref, gs, refs = refs[0], refs[1 : 1 + pieces], refs[1 + pieces :]
    sums, table, refs = refs[:4], refs[4], refs[5:]
    if has_after:
        (out_chunks, conv_chunks), refs = refs[:2], refs[2:]
    gw_out, gw_conv, g_gain3, g_shift3 = sums
    scratch = [refs[4 * q : 4 * q + 4] for q in range(group)]
    width, inner = w_out_t.shape
    step = pl.program_id(0)

    @pl.when(step == 0)
    def _():
        for k, ref in enumerate(sums):
            ref[...] = before[k][...] if has_before else jnp.zeros_like(ref)
        table[...] = jnp.zeros_like(table)
        for taps, act, _, _ in scratch:
            taps[3 * inner :, :] = jnp.ones_like(taps[3 * inner :, :])
            act[inner:, :] = jnp.ones_like(act[inner:, :])

    for q in range(group):
        taps, act, gc, gt = scratch[q]
        m = step * group + q
        base = m * REACH
        length = taps.shape[1]
        columns = length // LANES
        mid = mids[0][q] if pieces == 1 else jnp.concatenate([ref[q] for ref in mids], axis=1)
        lane = lax.broadcasted_iota(jnp.int32, (1, LANES), 1)
        if prompts:
            begin = chosen(base, lane, lane >= 0, batches)
            before_rows = tails[...]
        else:
            start = cont_start[m, 0, 1]
            owners = cont_map[m, 0, 0], cont_map[m, 0, 1]
            at_most = (length // LANES - 2) * LANES
            window = jnp.minimum(lax.shift_right_logical(start, 7) * LANES, at_most)
            window = pl.multiple_of(window, LANES)
            begin = chosen(base, lane, lane < start, batches)
            before_rows = tails[owners[0]]
        first = dot(before_rows, begin, 1, 0).astype(bf16)
        taps[0:inner, :] = mid
        one, two = shifted_right(mid, STEP), shifted_right(mid, REACH)
        if not prompts:
            row = lax.broadcasted_iota(jnp.int32, (1, length), 1)
            since = jnp.where(row < start, row, row - start)
            near_one = jnp.where(since >= STEP, 1.0, 0.0)
            near_two = jnp.where(since >= REACH, 1.0, 0.0)
            full = lambda w: jnp.broadcast_to(w, (inner, length)).astype(bf16)
            one, two = one * full(near_one), two * full(near_two)
        taps[inner : 2 * inner, :] = one
        taps[2 * inner : 3 * inner, :] = two
        taps[inner : 2 * inner, :LANES] += first[:, :LANES]
        taps[2 * inner : 3 * inner, :LANES] += first[:, LANES:]
        if not prompts:
            wide = pl.ds(window, 2 * LANES)
            offset = window + lax.broadcasted_iota(jnp.int32, (1, 2 * LANES), 1) - start
            later = chosen(base, offset, offset >= 0, batches)
            far = dot(tails[owners[1]], later, 1, 0).astype(bf16)
            taps[inner : 2 * inner, wide] += far[:, : 2 * LANES]
            taps[2 * inner : 3 * inner, wide] += far[:, 2 * LANES :]
        cot = cot_ref[q, 0]
        conv = dot(w_conv_t[...], taps[0 : 3 * inner, :], 1, 0)
        g_act = dot(w_out[...], cot, 1, 0)
        for c in range(columns):
            normed, scale = normed_of(conv[:, at(c)] + vec3[0])
            value, slope = silu_and_slope(normed * vec3[1] + vec3[2])
            act[0:inner, at(c)] = value.astype(bf16)
            g = g_act[:, at(c)] * slope
            gn, g_in = norm_backward(g, normed, scale, vec3[1])
            g_gain3[...] += gn
            g_shift3[...] += g
            gc[:, at(c)] = g_in.astype(bf16)
        branch = dot(w_out_t[...], act[0:inner, :], 1, 0)
        for c in range(columns):
            y = x_ref[q, 0, :, at(c)].astype(f32) + (branch[:, at(c)] + bias_out[...])
            out_ref[q, 0, :, at(c)] = y.astype(bf16)
        gw_out[...] += dot(cot, act[...], 1, 1)
        gw_conv[...] += dot(gc[...], taps[...], 1, 1)
        g_taps = dot(w_conv[...], gc[...], 1, 0)
        g0, g1, g2 = (g_taps[k * inner : (k + 1) * inner] for k in range(3))
        both = jnp.concatenate([g1[:, :LANES], g2[:, :LANES]], axis=1).astype(bf16)
        back = dot(both, begin, 1, 1)
        if prompts:
            table[...] += back
        else:
            table[owners[0]] += back
            gt[0] = g1.astype(bf16)
            gt[1] = g2.astype(bf16)
            both = jnp.concatenate([gt[0, :, wide], gt[1, :, wide]], axis=1)
            table[owners[1]] += dot(both, later, 1, 1)
            g1, g2 = g1 * near_one, g2 * near_two
        g_mid = (g0 + shifted_left(g1, STEP) + shifted_left(g2, REACH)).astype(bf16)
        if pieces == 1:
            gs[0][q] = g_mid
        else:
            gs[0][q] = g_mid[:, : length - LANES]
            gs[1][q] = g_mid[:, length - LANES :]

    if has_after:

        @pl.when(step == pl.num_programs(0) - 1)
        def _():
            count, few, _ = conv_chunks.shape
            many = out_chunks.shape[1]
            gw_conv[:, 3 * inner + 1 : 3 * inner + 2] = jnp.sum(g_gain3[...], axis=1, keepdims=True)
            gw_conv[:, 3 * inner + 2 : 3 * inner + 3] = jnp.sum(g_shift3[...], axis=1, keepdims=True)
            for r in range(count):
                out_chunks[r] = gw_out[r * many : (r + 1) * many, : inner + 1]
                conv_chunks[r] = gw_conv[r * few : (r + 1) * few, : 3 * inner + 3]


def middle(prompts, group, scalars, mids, x, cot, tails, weights, before=None, chunks=0):
    batches, _, width, length = x.shape
    inner = mids[0].shape[1]
    block = lambda a: blocks(a.shape, a.shape[-1], group, 0)
    args = list(scalars) + mids + [x, cot, tails] + list(weights) + list(before or ())
    in_specs = [pl.BlockSpec(memory_space=pltpu.SMEM)] * len(scalars)
    in_specs += [block(a) for a in mids + [x, cot]]
    in_specs += [WHOLE] * (len(args) - len(in_specs))
    out_like = [jax.ShapeDtypeStruct(x.shape, bf16)]
    out_like += [jax.ShapeDtypeStruct(mid.shape, bf16) for mid in mids]
    sums = [
        (width, inner + 16),
        (inner, 3 * inner + 16),
        (inner, LANES),
        (inner, LANES),
        tails.shape,
    ]
    if chunks:
        sums += [(chunks, width // chunks, inner + 1), (chunks, inner // chunks, 3 * inner + 3)]
    scratch = []
    for _ in range(group):
        scratch += [
            pltpu.VMEM((3 * inner + 16, length), bf16),
            pltpu.VMEM((inner + 16, length), bf16),
            pltpu.VMEM((inner, length), bf16),
            pltpu.VMEM((2, inner, length), bf16),
        ]
    return pl.pallas_call(
        functools.partial(
            middle_kernel, batches, prompts, group, len(mids), before is not None, chunks > 0
        ),
        grid=(batches // group,),
        in_specs=in_specs,
        out_specs=[block(a) for a in out_like] + [WHOLE] * len(sums),
        out_shape=out_like + [jax.ShapeDtypeStruct(shape, f32) for shape in sums],
        scratch_shapes=scratch,
        compiler_params=PARAMS,
        cost_estimate=cost(batches * length * 9 * inner * width, 3 * x.size * 2),
        name="middle",
    )(*args)


def back_kernel(has_rim, has_before, has_into, has_after, *refs):
    (x_ref, cot_ref, g_ref, n2_ref, r2_ref), refs = refs[:5], refs[5:]
    (w_in, vec1, vec2), refs = refs[:3], refs[3:]
    if has_rim:
        rim, refs = refs[0], refs[1:]
    if has_before:
        before, refs = refs[:5], refs[5:]
    if has_into:
        refs = refs[1:]
    out_ref, sums, refs = refs[0], refs[1:6], refs[6:]
    if has_after:
        (in_chunks, one_chunks), refs = refs[:2], refs[2:]
    act, gh = refs
    gw_in, g_gain2, g_shift2, g_gain1, g_shift1 = sums
    width, inner = w_in.shape
    step = pl.program_id(0)

    @pl.when(step == 0)
    def _():
        for k, ref in enumerate(sums):
            ref[...] = before[k][...] if has_before else jnp.zeros_like(ref)
        act[width:, :] = jnp.ones_like(act[width:, :])

    columns = columns_in(x_ref)
    for c in range(columns):
        normed = column_of(n2_ref, c).astype(f32)
        _, slope = silu_and_slope(normed * vec2[1] + vec2[2])
        g = column_of(g_ref, c).astype(f32)
        if has_rim:
            piece = rim[:, c * REACH : (c + 1) * REACH]
            g += jnp.concatenate([jnp.zeros((inner, LANES - REACH), f32), piece], axis=1)
        g = g * slope
        gn, g_in = norm_backward(g, normed, column_of(r2_ref, c), vec2[1])
        g_gain2[...] += gn
        g_shift2[...] += g
        gh[:, at(c)] = g_in.astype(bf16)
    g_act = dot(w_in[...], gh[...], 1, 0)
    for c in range(columns):
        normed, scale = normed_of(column_of(x_ref, c).astype(f32))
        value, slope = silu_and_slope(normed * vec1[0] + vec1[1])
        act[0:width, at(c)] = value.astype(bf16)
        g = g_act[:, at(c)] * slope
        gn, g_in = norm_backward(g, normed, scale, vec1[0])
        g_gain1[...] += gn
        g_shift1[...] += g
        put_column(out_ref, c, column_of(cot_ref, c).astype(f32) + g_in)
    gw_in[...] += dot(gh[...], act[...], 1, 1)

    if has_after:

        @pl.when(step == pl.num_programs(0) - 1)
        def _():
            count, few, _ = in_chunks.shape
            many = one_chunks.shape[1]
            gw_in[:, width + 1 : width + 2] = jnp.sum(g_gain2[...], axis=1, keepdims=True)
            gw_in[:, width + 2 : width + 3] = jnp.sum(g_shift2[...], axis=1, keepdims=True)
            g_gain1[:, 0:1] = jnp.sum(g_gain1[...], axis=1, keepdims=True)
            g_gain1[:, 1:2] = jnp.sum(g_shift1[...], axis=1, keepdims=True)
            for r in range(count):
                in_chunks[r] = gw_in[r * few : (r + 1) * few, : width + 3]
                one_chunks[r] = g_gain1[r * many : (r + 1) * many, 0:2]


def back(x, cot, g, n2, r2, part, w_in, vec1, vec2, rim=None, before=None, into=None, chunks=0):
    width, inner = w_in.shape
    batches = x.shape[0]
    lanes, group, first = part
    block = blocks(x.shape, lanes, group, first)
    in_specs = [block, block] + [blocks(a.shape, lanes, group, 0) for a in (g, n2, r2)] + [WHOLE] * 3
    args = [x, cot, g, n2, r2, w_in, vec1, vec2]
    if rim is not None:
        args.append(rim)
        in_specs.append(pl.BlockSpec((inner, GROUP * REACH), lambda i: (0, i)))
    if before is not None:
        args += before
        in_specs += [WHOLE] * 5
    aliases = {}
    if into is not None:
        aliases = {len(args): 0}
        args.append(into)
        in_specs.append(pl.BlockSpec(memory_space=pl.ANY))
    sums = [(inner, width + 16), (inner, LANES), (inner, LANES), (width, LANES), (width, LANES)]
    if chunks:
        sums += [(chunks, inner // chunks, width + 3), (chunks, width // chunks, 2)]
    return pl.pallas_call(
        functools.partial(
            back_kernel, rim is not None, before is not None, into is not None, chunks > 0
        ),
        grid=(batches // group,),
        in_specs=in_specs,
        out_specs=[block] + [WHOLE] * len(sums),
        out_shape=[jax.ShapeDtypeStruct(x.shape, f32)]
        + [jax.ShapeDtypeStruct(shape, f32) for shape in sums],
        scratch_shapes=[
            pltpu.VMEM((width + 16, group * lanes), bf16),
            pltpu.VMEM((inner, group * lanes), bf16),
        ],
        input_output_aliases=aliases,
        compiler_params=PARAMS,
        cost_estimate=cost(10 * width * inner * batches * lanes, 0),
        name="back",
    )(*args)


def passed_along(x, axis, by):
    size = lax.axis_size(axis)
    pairs = [(i, i + by) for i in range(size) if 0 <= i + by < size]
    return lax.ppermute(x, axis, pairs)


def gathered(x, axis):
    size = lax.axis_size(axis)
    if size > 4:
        return lax.all_gather(x, axis)
    me = lax.axis_index(axis)
    total = jnp.zeros((size,) + x.shape, x.dtype)
    for k in range(size):
        piece = x if k == 0 else lax.ppermute(x, axis, [(i, i ^ k) for i in range(size)])
        total = lax.dynamic_update_index_in_dim(total, piece, me ^ k, 0)
    return total


def sent_from_last(x, axis):
    size = lax.axis_size(axis)
    me = lax.axis_index(axis)
    value = x
    for j in range(size - 1):
        piece = lax.ppermute(x, axis, [(size - 1, j)])
        value = jnp.where(me == j, piece, value)
    return value


def summed_at_last(x, axis):
    size = lax.axis_size(axis)
    total = x.astype(f32)
    for j in range(size - 1):
        total = total + lax.ppermute(x, axis, [(j, size - 1)]).astype(f32)
    return total


def on_device(
    prompt_x,
    cont_x,
    cont_map,
    cont_start,
    w_in,
    w_conv,
    w_out,
    norm1_gain,
    norm1_bias,
    bias_in,
    norm2_gain,
    norm2_bias,
    bias_conv,
    norm3_gain,
    norm3_bias,
    bias_out,
    prompt_cot,
    cont_cot,
):
    inner = w_conv.shape[2]
    turned = lambda a: jnp.swapaxes(a, 2, 3)
    prompt_x, cont_x, prompt_cot, cont_cot = map(turned, (prompt_x, cont_x, prompt_cot, cont_cot))
    width = prompt_x.shape[2]
    shards, reps = lax.axis_size("shard"), lax.axis_size("rep")
    is_last = lax.axis_index("shard") == shards - 1
    low_in = gathered(w_in.astype(bf16), "shard").reshape(width, inner)
    own = w_out.shape[0]
    packed = jnp.concatenate(
        [w_conv.reshape(3 * own, inner), w_out[:, :inner], w_out[:, inner:]], axis=0
    ).astype(bf16)
    packed = gathered(packed, "shard")
    low_conv = packed[:, : 3 * own].reshape(shards, 3, own, inner).transpose(1, 0, 2, 3)
    low_conv = low_conv.reshape(3 * inner, inner)
    low_out = packed[:, 3 * own :].reshape(shards, 2, own, inner).transpose(0, 2, 1, 3)
    low_out = low_out.reshape(inner, width)
    spread = lambda *v: jnp.broadcast_to(jnp.stack(v)[:, :, None], (len(v), v[0].shape[0], LANES))
    vec1 = spread(norm1_gain, norm1_bias)
    vec2 = spread(bias_in, norm2_gain, norm2_bias)
    vec3 = spread(bias_conv, norm3_gain, norm3_bias)
    vec_out = spread(bias_out)[0]

    rows_p, rows_c = prompt_x.shape[3], cont_x.shape[3]
    last = (LANES, GROUP, rows_p - LANES)
    rest = (rows_p - LANES, 1, 0)
    every = (rows_c, 1, 0)
    have_first = rows_p > LANES
    w_in_t = low_in.T
    mid_l, n2_l, r2_l, rim = front([prompt_x], [last], w_in_t, vec1, vec2, with_rim=True)
    halo = passed_along(rim, "shard", 1)
    tails = lax.all_gather(sent_from_last(rim, "shard"), "rep", axis=0)
    if have_first:
        mid_f, n2_f, r2_f, mid_c, n2_c, r2_c = front(
            [prompt_x, cont_x], [rest, every], w_in_t, vec1, vec2
        )
        mids = [mid_f, mid_l]
    else:
        mid_c, n2_c, r2_c = front([cont_x], [every], w_in_t, vec1, vec2)
        mids = [mid_l]

    weights = (low_conv.T, low_conv, low_out.T, low_out, vec3, vec_out)
    prompt_out, *results = middle(True, 1, [], mids, prompt_x, prompt_cot, halo, weights)
    g_ps, results = results[: len(mids)], results[len(mids) :]
    sums, rim_out = results[:4], results[4]
    cont_out, g_c, *sums, table, out_chunks, conv_chunks = middle(
        False,
        1,
        [cont_start, cont_map],
        [mid_c],
        cont_x,
        cont_cot,
        tails,
        weights,
        before=sums,
        chunks=reps,
    )
    back_rim = passed_along(rim_out.astype(bf16), "shard", -1).astype(f32)
    own_tail = lax.psum_scatter(table, "rep", scatter_dimension=0)
    own_tail = summed_at_last(own_tail.astype(bf16), "shard")
    rim_in = back_rim + jnp.where(is_last, own_tail, 0.0)
    out_chunks = lax.psum_scatter(out_chunks, "rep", scatter_dimension=0)
    conv_chunks = lax.psum_scatter(conv_chunks, "rep", scatter_dimension=0)

    sums = None
    prompt_grad = None
    if have_first:
        prompt_grad, *sums = back(
            prompt_x, prompt_cot, g_ps[0], n2_f, r2_f, rest, low_in, vec1, vec2
        )
    cont_grad, *sums = back(
        cont_x, cont_cot, g_c, n2_c, r2_c, every, low_in, vec1, vec2, before=sums
    )
    prompt_grad, *results = back(
        prompt_x,
        prompt_cot,
        g_ps[-1],
        n2_l,
        r2_l,
        last,
        low_in,
        vec1,
        vec2,
        rim=rim_in,
        before=sums,
        into=prompt_grad,
        chunks=reps,
    )
    in_chunks, one_chunks = results[5:]
    swapped = lambda a, axis: lax.all_to_all(a.astype(bf16), axis, 0, 0, tiled=True).astype(f32)
    in_chunks = jnp.sum(swapped(in_chunks, "rep"), axis=0)
    one_chunks = jnp.sum(swapped(one_chunks, "rep"), axis=0)

    few = inner // reps
    twice = width // inner
    halves = lambda a: jnp.concatenate(jnp.split(a, twice, axis=0), axis=1)
    part_out = halves(out_chunks)
    kept = [part_out[:, h * (inner + 1) + inner][:, None] for h in range(twice)]
    kept += [halves(one_chunks), conv_chunks[:, 3 * inner :], in_chunks[:, width:]]
    kept = jnp.concatenate(kept, axis=1)
    pieces = []
    for j in range(shards):
        wide = width // shards
        parts = [part_out[:, h * (inner + 1) + j * own :][:, :own] for h in range(twice)]
        parts += [conv_chunks[:, k * inner + j * own :][:, :own] for k in range(3)]
        parts += [in_chunks[:, j * wide : (j + 1) * wide], kept]
        pieces.append(jnp.concatenate(parts, axis=1))
    mine = jnp.sum(swapped(jnp.stack(pieces), "shard"), axis=0)
    whole = lax.all_gather(mine, "rep")
    a, b, c = twice * own, (twice + 3) * own, (twice + 3) * own + width // shards
    grad_w_out = whole[:, :, :a].reshape(reps, few, twice, own).transpose(3, 0, 2, 1)
    grad_w_out = grad_w_out.reshape(own, width)
    grad_w_conv = whole[:, :, a:b].reshape(inner, 3, own).transpose(1, 2, 0)
    grad_w_in = whole[:, :, b:c].reshape(inner, width // shards).T
    small = whole[:, :, c:]
    by_width = lambda v: v.transpose(0, 2, 1).reshape(width)
    grad_bias_out = by_width(small[:, :, :twice])
    ones = small[:, :, twice : 3 * twice].reshape(reps, few, twice, 2)
    grad_gain1, grad_shift1 = by_width(ones[..., 0]), by_width(ones[..., 1])
    by_inner = [small[:, :, 3 * twice + k].reshape(inner) for k in range(6)]
    grad_bias_conv, grad_gain3, grad_shift3, grad_bias_in, grad_gain2, grad_shift2 = by_inner
    return (
        turned(prompt_out),
        turned(cont_out),
        turned(prompt_grad),
        turned(cont_grad),
        grad_w_in,
        grad_w_conv,
        grad_w_out,
        grad_gain1,
        grad_shift1,
        grad_bias_in,
        grad_gain2,
        grad_shift2,
        grad_bias_conv,
        grad_gain3,
        grad_shift3,
        grad_bias_out,
    )


def solution(mesh):
    rows = P(None, "rep", "shard", None)
    buffers = P(None, ("rep", "shard"), None, None)
    in_specs = (
        rows,
        buffers,
        P(None, ("rep", "shard"), None),
        P(None, ("rep", "shard"), None),
        P("shard", None),
        P(None, "shard", None),
        P("shard", None),
    ) + (P(),) * 9 + (rows, buffers)
    out_specs = (
        rows,
        buffers,
        rows,
        buffers,
        P("shard", None),
        P(None, "shard", None),
        P("shard", None),
    ) + (P(),) * 9
    return jax.shard_map(
        on_device, mesh=mesh, in_specs=in_specs, out_specs=out_specs, check_vma=False
    )
```

time: 968 us -> 446 us (0.46)
  other arithmetic: 262 us -> 11.9 us
  Pallas kernels: 0 us -> 204 us
  local copies, waits for them, and re-layouts: 205 us -> 41.5 us
  matrix products: 151 us -> 0 us
  blocking collectives: 138 us -> 12.7 us
  waiting for transfers between devices: 179 us -> 115 us
  starting transfers between devices: 6.18 us -> 38.9 us
    pallas_call x0 -> x7, Pallas kernels: none -> 204 us  [the longest x2 87 us: middle(): pl.pallas_call(functools.partial(middle_kernel, batches, prompts, group,...]
    dot_general x9 -> x0, matrix products: 151 us -> none  [the longest x1 26 us: on_device(): jnp.einsum('mre,de->mrd', grad_hidden_low, back_in, preferred_element_typ...]
    psum x3 -> x0, waiting for transfers between devices: 141 us -> none  [the longest x1 92.6 us: on_device(): lax.psum((tail_part, part_bias_conv, part_gain_three, part_shift_three, p...]
    gather x4 -> x0, local copies, waits for them, and re-layouts: 108 us -> none  [pick_rows(): block[where_from]]
    reduce_sum x10 -> x3, other arithmetic: 89.6 us -> 0.86 us  [the longest x1 0.72 us: on_device(): mine = jnp.sum(swapped(jnp.stack(pieces), 'shard'), axis=0)]
    all_gather x3 -> x0, blocking collectives: 67.5 us -> none  [the longest x1 28.1 us: on_device(): lax.all_gather(w_conv.astype(jnp.bfloat16), 'shard', axis=1, tiled=True)]
    unnamed x12 -> x0, other arithmetic: 63.2 us -> none
    unnamed x142 -> x45, local copies, waits for them, and re-layouts: 51.5 us -> 6.19 us
  transfers between devices with their start and end apart: 9 -> 21, of which waited for: 5 -> 8; matrix products, arithmetic and copies ran while one was open for 33% -> 7% of each run, Pallas kernels for 0% -> 36%
where the time goes in v1:
time: 446 us; the launch traced here: 439 us
  Pallas kernels  204 us (46%)
  waiting for transfers between devices  115 us (26%)
  local copies, waits for them, and re-layouts  41.5 us (9%)
  starting transfers between devices  38.9 us (9%)
  between operations  14.7 us (3%)
  blocking collectives  12.7 us (3%)
  other arithmetic  11.9 us (3%)
    pallas_call x2, Pallas kernels, middle(): pl.pallas_call(functools.partial(middle_kernel, batches, prompts, group,...  87 us
    pallas_call x3, Pallas kernels, back(): pl.pallas_call(functools.partial(back_kernel, rim is not None, before is...  81.7 us
    ppermute x6, waiting for transfers between devices, gathered(): lax.ppermute(x, axis, [(i, i ^ k) for i in range(size)])  41.5 us
    pallas_call x2, Pallas kernels, front(): pl.pallas_call(functools.partial(front_kernel, len(xs), with_rim), grid=(...  35.2 us
    all_gather x1, waiting for transfers between devices, on_device(): whole = lax.all_gather(mine, 'rep')  24.7 us
    reduce_scatter x1, waiting for transfers between devices, on_device(): own_tail = lax.psum_scatter(table, 'rep', scatter_dimension=0)  21 us
    ppermute x6, starting transfers between devices, gathered(): lax.ppermute(x, axis, [(i, i ^ k) for i in range(size)])  14.4 us
    all_to_all x1, blocking collectives, on_device(): lax.all_to_all(a.astype(bf16), axis, 0, 0, tiled=True).astype(f32)  12.7 us
  transfers between devices with their start and end apart: 21, of which 8 were waited for; matrix products, arithmetic and copies ran while one was open for 7% of the time, Pallas kernels for 36%

profile of v1, /device:TPU:0, one launch (start us, length us, event | category | flops | bytes accessed | tf_op | source)
XLA Modules:
  0.0 439.3 jit_solution(9218324305727521429)
XLA Ops:
  7.2 1.1 fusion.3
  8.4 1.2 convert.116
  10.8 5.0 %collective-permute-start.6 = (bf16[500,400]{1,0:T(8,128)(2,1)}, bf16[500,400]{1,0:T(8,128)(2,1)}, u32[]{:S(2)}, u32[]{:S(2)}) collective-permute-start(bf16[500,400]{1,0:T(8,128)(2,1)} %pad_maximum_fusion), channel_id=1, source_target_pairs={{0,3},{1,2},{2,1},{3,0},{4,7},{5,6},{6,5},{7,4},{8,11},{9,10},{10,... | collective-permute-start | bytes 1200008 | tf_op jit(solution)/shard_map/ppermute | solution.py:435
  17.2 1.5 collective-permute-start
  18.7 2.4 collective-permute-start.2
  22.9 25.7 %collective-permute-done = bf16[200,400]{1,0:T(8,128)(2,1)} collective-permute-done((bf16[200,400]{1,0:T(8,128)(2,1)}, bf16[200,400]{1,0:T(8,128)(2,1)}, u32[]{:S(2)}, u32[]{:S(2)}) %collective-permute-start) | collective-permute-done | bytes 160032 | tf_op jit(solution)/shard_map/ppermute | solution.py:435
  49.5 1.0 bitcast_dynamic-update-slice_fusion.4
  50.4 1.9 collective-permute-done.2
  53.3 1.2 copy.170.refs_2_.refs_1_
  54.5 1.0 broadcast_in_dim.61.refs_4_.refs_3_.refs_7_
  55.6 1.2 broadcast_in_dim.60.refs_3_.refs_2_.refs_6_
  56.7 6.3 %front.3 = (bf16[8,400,128]{2,1,0:T(8,128)(2,1)}, bf16[8,400,128]{2,1,0:T(8,128)(2,1)}, f32[8,1,128]{2,1,0:T(1,128)}, bf16[400,256]{1,0:T(8,128)(2,1)}) custom-call(bf16[8,1,800,512]{3,2,1,0:T(8,128)(2,1)} %bitcast.79, bf16[400,800]{1,0:T(8,128)(2,1)} %copy.170.refs_2_.refs_1_, f32[2,800,128]{2,1,0:T(8,128)} %broadcast_in_dim.60.refs_3_.refs_2_.refs_6_, ...), custom_call_target="tpu_custom_call" | custom-call | flops 3276800000 | tf_op jit(solution)/shard_map/front/pallas_call | solution.py:128
  63.0 1.3 collective-permute-start.9
  65.7 28.9 %front.2 = (bf16[8,400,384]{2,1,0:T(8,128)(2,1)}, bf16[8,400,384]{2,1,0:T(8,128)(2,1)}, f32[8,1,384]{2,1,0:T(1,128)}, bf16[8,400,512]{2,1,0:T(8,128)(2,1)}, bf16...) custom-call(bf16[8,1,800,512]{3,2,1,0:T(8,128)(2,1)} %bitcast.80, bf16[8,1,800,512]{3,2,1,0:T(8,128)(2,1)} %bitcast.110, ...), custom_call_target="tpu_custom_call" | custom-call | flops 22937600000 | tf_op jit(solution)/shard_map/front/pallas_call | solution.py:128
  94.7 4.9 %collective-permute-start.5 = (bf16[500,400]{1,0:T(8,128)(2,1)}, bf16[500,400]{1,0:T(8,128)(2,1)S(1)}, u32[]{:S(2)}, u32[]{:S(2)}) collective-permute-start(bf16[500,400]{1,0:T(8,128)(2,1)} %pad_maximum_fusion), channel_id=1, source_target_pairs={{0,2},{1,3},{2,0},{3,1},{4,6},{5,7},{6,4},{7,5},{8,10},{9,11},{10,... | collective-permute-start | bytes 1200008 | tf_op jit(solution)/shard_map/ppermute | solution.py:435
  99.6 5.8 %collective-permute-start.3 = (bf16[400,256]{1,0:T(8,128)(2,1)S(1)}, bf16[400,256]{1,0:T(8,128)(2,1)}, u32[]{:S(2)}, u32[]{:S(2)}) collective-permute-start(bf16[400,256]{1,0:T(8,128)(2,1)S(1)} %copy-done.7), channel_id=1, source_target_pairs={{0,1},{1,2},{2,3},{4,5},{5,6},{6,7},{8,9},{9,10},{10,11},{12,13},{... | collective-permute-start | bytes 614408 | tf_op jit(solution)/shard_map/ppermute | solution.py:425
  106.8 1.1 bitcast_dynamic-update-slice_fusion.2
  107.8 13.9 %collective-permute-done.5 = bf16[500,400]{1,0:T(8,128)(2,1)S(1)} collective-permute-done((bf16[500,400]{1,0:T(8,128)(2,1)}, bf16[500,400]{1,0:T(8,128)(2,1)S(1)}, u32[]{:S(2)}, u32[]{:S(2)}) %collective-permute-start.5) | collective-permute-done | bytes 400032 | tf_op jit(solution)/shard_map/ppermute | solution.py:435
  121.8 1.2 bitcast_dynamic-update-slice_fusion
  123.0 1.1 slice.253
  124.7 1.3 copy.174
  128.3 1.2 copy.177.refs_7_.refs_8_
  129.5 1.5 copy.176.refs_6_.refs_7_
  131.9 1.1 broadcast_in_dim.66.refs_9_.refs_10_
  133.0 39.0 %middle.2 = (bf16[8,1,800,512]{3,2,1,0:T(8,128)(2,1)}, bf16[8,400,384]{2,1,0:T(8,128)(2,1)}, bf16[8,400,128]{2,1,0:T(8,128)(2,1)}, f32[800,416]{1,0:T(8,128)}, f...) custom-call(bf16[8,400,384]{2,1,0:T(8,128)(2,1)} %get-tuple-element.54.refs_0_, ...), custom_call_target="tpu_custom_call" | custom-call | flops 29491200000 | bytes 19660800 | tf_op jit(solution)/shard_map/middle/pallas_call | solution.py:303
  172.1 47.9 %middle.3 = (bf16[8,1,800,512]{3,2,1,0:T(8,128)(2,1)}, bf16[8,400,512]{2,1,0:T(8,128)(2,1)}, f32[800,416]{1,0:T(8,128)}, f32[400,1216]{1,0:T(8,128)}, f32[400,12...) custom-call(s32[8,1,2]{2,1,0:T(1,128)} %copy.178.refs_0_, ...), custom_call_target="tpu_custom_call" | custom-call | flops 29491200000 | bytes 19660800 | tf_op jit(solution)/shard_map/middle/pallas_call | solution.py:303
  221.1 1.3 collective-permute-start.10
  222.4 29.0 %back.3 = (f32[8,1,800,512]{3,2,1,0:T(8,128)}, f32[400,816]{1,0:T(8,128)}, f32[400,128]{1,0:T(8,128)}, f32[400,128]{1,0:T(8,128)}, f32[800,128]{1,0:T(8,128)}, /*index=5*/f32[800,128]{1,0:T(8,128)}) custom-call(bf16[8,1,800,512]{3,2,1,0:T(8,128)(2,1)} %bitcast.82, bf16[8,1,800,512]{3,2,1,0:T(8,128)(2,1)} %bitcast.85, ...), custom_call_target="tpu_custom_call" | custom-call | flops 24576000000 | tf_op jit(solution)/shard_map/back/pallas_call | solution.py:402
  251.4 37.7 %back.4 = (f32[8,1,800,512]{3,2,1,0:T(8,128)}, f32[400,816]{1,0:T(8,128)}, f32[400,128]{1,0:T(8,128)}, f32[400,128]{1,0:T(8,128)}, f32[800,128]{1,0:T(8,128)}, /*index=5*/f32[800,128]{1,0:T(8,128)}) custom-call(bf16[8,1,800,512]{3,2,1,0:T(8,128)(2,1)} %bitcast.112, bf16[8,1,800,512]{3,2,1,0:T(8,128)(2,1)} %bitcast.114, ...), custom_call_target="tpu_custom_call" | custom-call | flops 32768000000 | tf_op jit(solution)/shard_map/back/pallas_call | solution.py:402
  289.1 1.0 slice_bitcast_fusion.1
  290.2 21.0 %reduce-scatter.4.cloned.1.call-done = f32[1,400,256]{2,1,0:T(8,128)} async-done(((f32[8,400,256]{2,1,0:T(8,128)}), f32[1,400,256]{2,1,0:T(8,128)}) %reduce-scatter.4.cloned.1.call-update) | async-done | bytes 409616 | tf_op jit(solution)/shard_map/reduce_scatter | solution.py:535
  311.2 1.0 convert_bitcast_fusion
  312.9 5.9 %collective-permute-start.11 = (bf16[400,256]{1,0:T(8,128)(2,1)S(1)}, bf16[400,256]{1,0:T(8,128)(2,1)S(1)}, u32[]{:S(2)}, u32[]{:S(2)}) collective-permute-start(bf16[400,256]{1,0:T(8,128)(2,1)S(1)} %convert_bitcast_fusion), channel_id=1, source_target_pairs={{0,3},{4,7},{8,11},{12,15},{16,19},{20,23},{24,27},{28,31}} | collective-permute-start | bytes 614408 | tf_op jit(solution)/shard_map/ppermute | solution.py:454
  319.6 3.6 collective-permute-done.11
  323.2 1.9 select_add_fusion.refs_8_
  325.1 15.1 %back.5 = (f32[8,1,800,512]{3,2,1,0:T(8,128)}, f32[400,816]{1,0:T(8,128)}, f32[400,128]{1,0:T(8,128)}, f32[400,128]{1,0:T(8,128)}, f32[800,128]{1,0:T(8,128)}, /...) custom-call(bf16[8,1,800,512]{3,2,1,0:T(8,128)(2,1)} %bitcast.83, ...), custom_call_target="tpu_custom_call", output_to_operand_aliasing={{0}: (14, {})} | custom-call | flops 8192000000 | tf_op jit(solution)/shard_map/back/pallas_call | solution.py:402
  340.2 1.0 convert_element_type.62
  342.0 3.3 all-to-all-start.1
  345.3 11.7 %reduce-scatter.8.cloned.1.call-done = f32[1,50,1203]{2,1,0:T(8,128)} async-done(((f32[8,50,1203]{2,1,0:T(8,128)}), f32[1,50,1203]{2,1,0:T(8,128)}) %reduce-scatter.8.cloned.1.call-update) | async-done | bytes 240616 | tf_op jit(solution)/shard_map/reduce_scatter | solution.py:539
  357.0 1.0 bitcast_convert_fusion
  358.8 2.4 convert_element_type.60
  361.2 3.5 all-to-all-start
  365.3 12.2 %all-to-all-done = bf16[8,50,803]{2,1,0:T(8,128)(2,1)S(1)} async-done(((bf16[8,50,803]{2,1,0:T(8,128)(2,1)}), bf16[8,50,803]{2,1,0:T(8,128)(2,1)S(1)}, u32[]{:S(2)}, u32[]{:S(2)}) %all-to-all-start) | async-done | bytes 642432 | tf_op jit(solution)/shard_map/all_to_all | solution.py:566
  378.5 12.7 %all_to_all.15 = bf16[4,50,712]{2,1,0:T(8,128)(2,1)S(1)} all-to-all(bf16[4,50,712]{2,1,0:T(8,128)(2,1)S(1)} %pad_maximum_fusion.1), channel_id=1, replica_groups=mesh['rep'=8,'shard'=4] {'shard'}, dimensions={0} | all-to-all | bytes 569600 | tf_op jit(solution)/shard_map/all_to_all | solution.py:566
  391.9 24.7 %all-gather.8.cloned.1.call-done = f32[8,50,712]{2,1,0:T(8,128)} async-done(((f32[1,50,712]{2,1,0:T(8,128)}), f32[8,50,712]{2,1,0:T(8,128)}) %all-gather.8.cloned.1.call-update) | async-done | bytes 1139216 | tf_op jit(solution)/shard_map/all_gather | solution.py:585
  416.6 2.7 slice_reduce_fusion
  423.3 1.1 slice.285
  429.6 1.9 reshape.150
  (136 shorter events, 29.1 us)
Async XLA Ops:
  7.2 164.9 %all-gather.6.cloned.1.call-start = ((), (), s32[]{:S(2)}) async-start(), calls=%async_computation.9 | async-start | bytes 1843200 | tf_op jit(solution)/shard_map/all_gather | solution.py:508
  8.4 7.6 %copy-start.6 = (f32[200,400]{1,0:T(8,128)S(1)}, f32[200,400]{1,0:T(8,128)}, u32[]{:S(2)}) copy-start(f32[200,400]{1,0:T(8,128)} %param.22) | copy-start | bytes 960004
  9.5 11.5 %copy-start.9 = (f32[800]{0:T(1024)S(1)}, f32[800]{0:T(1024)}, u32[]{:S(2)}) copy-start(f32[800]{0:T(1024)} %param.25) | copy-start | bytes 9604
  9.6 11.5 %copy-start.10 = (f32[800]{0:T(1024)S(1)}, f32[800]{0:T(1024)}, u32[]{:S(2)}) copy-start(f32[800]{0:T(1024)} %param.26) | copy-start | bytes 9604
  9.6 11.5 %copy-start.11 = (f32[400]{0:T(512)S(1)}, f32[400]{0:T(512)}, u32[]{:S(2)}) copy-start(f32[400]{0:T(512)} %param.29) | copy-start | bytes 4804
  9.6 11.5 %copy-start.12 = (f32[400]{0:T(512)S(1)}, f32[400]{0:T(512)}, u32[]{:S(2)}) copy-start(f32[400]{0:T(512)} %param.28) | copy-start | bytes 4804
  9.6 11.5 %copy-start.13 = (f32[400]{0:T(512)S(1)}, f32[400]{0:T(512)}, u32[]{:S(2)}) copy-start(f32[400]{0:T(512)} %param.27) | copy-start | bytes 4804
  9.6 11.5 %copy-start.14 = (f32[400]{0:T(512)S(1)}, f32[400]{0:T(512)}, u32[]{:S(2)}) copy-start(f32[400]{0:T(512)} %param.32) | copy-start | bytes 4804
  9.6 11.5 %copy-start.15 = (f32[400]{0:T(512)S(1)}, f32[400]{0:T(512)}, u32[]{:S(2)}) copy-start(f32[400]{0:T(512)} %param.31) | copy-start | bytes 4804
  9.6 11.5 %copy-start.16 = (f32[400]{0:T(512)S(1)}, f32[400]{0:T(512)}, u32[]{:S(2)}) copy-start(f32[400]{0:T(512)} %param.30) | copy-start | bytes 4804
  9.9 11.4 %copy-start.17 = (s32[8,1,2]{0,2,1:T(2,128)S(1)}, s32[8,1,2]{0,2,1:T(2,128)}, u32[]{:S(2)}) copy-start(s32[8,1,2]{0,2,1:T(2,128)} %param.20) | copy-start | bytes 196
  9.9 12.1 %copy-start.18 = (s32[8,1,2]{0,2,1:T(2,128)S(1)}, s32[8,1,2]{0,2,1:T(2,128)}, u32[]{:S(2)}) copy-start(s32[8,1,2]{0,2,1:T(2,128)} %param.21) | copy-start | bytes 196
  10.8 111.0 %collective-permute-start.6 = (bf16[500,400]{1,0:T(8,128)(2,1)}, bf16[500,400]{1,0:T(8,128)(2,1)}, u32[]{:S(2)}, u32[]{:S(2)}) collective-permute-start(bf16[500,400]{1,0:T(8,128)(2,1)} %pad_maximum_fusion), channel_id=1, source_target_pairs={{0,3},{1,2},{2,1},{3,0},{4,7},{5,6},{6,5},{7,4},{8,11},{9,10},{10,... | collective-permute-start | bytes 1200008 | tf_op jit(solution)/shard_map/ppermute | solution.py:435
  15.9 90.9 %collective-permute-start.4 = (bf16[500,400]{1,0:T(8,128)(2,1)}, bf16[500,400]{1,0:T(8,128)(2,1)}, u32[]{:S(2)}, u32[]{:S(2)}) collective-permute-start(bf16[500,400]{1,0:T(8,128)(2,1)} %pad_maximum_fusion), channel_id=1, source_target_pairs={{0,1},{1,0},{2,3},{3,2},{4,5},{5,4},{6,7},{7,6},{8,9},{9,8},{10,11... | collective-permute-start | bytes 1200008 | tf_op jit(solution)/shard_map/ppermute | solution.py:435
  16.6 32.8 %collective-permute-start.1 = (bf16[200,400]{1,0:T(8,128)(2,1)}, bf16[200,400]{1,0:T(8,128)(2,1)}, u32[]{:S(2)}, u32[]{:S(2)}) collective-permute-start(bf16[200,400]{1,0:T(8,128)(2,1)} %get-tuple-element.195), channel_id=1, source_target_pairs={{0,2},{1,3},{2,0},{3,1},{4,6},{5,7},{6,4},{7,5},{8,10},{9,11},{10,... | collective-permute-start | bytes 480008 | tf_op jit(solution)/shard_map/ppermute | solution.py:435
  17.2 31.3 %collective-permute-start = (bf16[200,400]{1,0:T(8,128)(2,1)}, bf16[200,400]{1,0:T(8,128)(2,1)}, u32[]{:S(2)}, u32[]{:S(2)}) collective-permute-start(bf16[200,400]{1,0:T(8,128)(2,1)} %get-tuple-element.195), channel_id=1, source_target_pairs={{0,1},{1,0},{2,3},{3,2},{4,5},{5,4},{6,7},{7,6},{8,9},{9,8},{10,11... | collective-permute-start | bytes 480008 | tf_op jit(solution)/shard_map/ppermute | solution.py:435
  18.7 33.7 %collective-permute-start.2 = (bf16[200,400]{1,0:T(8,128)(2,1)}, bf16[200,400]{1,0:T(8,128)(2,1)}, u32[]{:S(2)}, u32[]{:S(2)}) collective-permute-start(bf16[200,400]{1,0:T(8,128)(2,1)} %get-tuple-element.195), channel_id=1, source_target_pairs={{0,3},{1,2},{2,1},{3,0},{4,7},{5,6},{6,5},{7,4},{8,11},{9,10},{10,... | collective-permute-start | bytes 480008 | tf_op jit(solution)/shard_map/ppermute | solution.py:435
  53.3 9.7 %copy-start.1 = (bf16[4,200,400]{2,1,0:T(8,128)(2,1)}, bf16[4,200,400]{2,1,0:T(8,128)(2,1)S(1)}, u32[]{:S(2)}) copy-start(bf16[4,200,400]{2,1,0:T(8,128)(2,1)S(1)} %bitcast_dynamic-update-slice_fusion.3) | copy-start | bytes 1920004
  63.0 31.6 %collective-permute-start.9 = (bf16[400,256]{1,0:T(8,128)(2,1)}, bf16[400,256]{1,0:T(8,128)(2,1)S(1)}, u32[]{:S(2)}, u32[]{:S(2)}) collective-permute-start(bf16[400,256]{1,0:T(8,128)(2,1)} %get-tuple-element.56), channel_id=1, source_target_pairs={{3,0},{7,4},{11,8},{15,12},{19,16},{23,20},{27,24},{31,28}} | collective-permute-start | bytes 614408 | tf_op jit(solution)/shard_map/ppermute | solution.py:445
  64.3 35.3 %collective-permute-start.8 = (bf16[400,256]{1,0:T(8,128)(2,1)}, bf16[400,256]{1,0:T(8,128)(2,1)S(1)}, u32[]{:S(2)}, u32[]{:S(2)}) collective-permute-start(bf16[400,256]{1,0:T(8,128)(2,1)} %get-tuple-element.56), channel_id=1, source_target_pairs={{3,1},{7,5},{11,9},{15,13},{19,17},{23,21},{27,25},{31,29}} | collective-permute-start | bytes 614408 | tf_op jit(solution)/shard_map/ppermute | solution.py:445
  65.0 40.4 %collective-permute-start.7 = (bf16[400,256]{1,0:T(8,128)(2,1)}, bf16[400,256]{1,0:T(8,128)(2,1)S(1)}, u32[]{:S(2)}, u32[]{:S(2)}) collective-permute-start(bf16[400,256]{1,0:T(8,128)(2,1)} %get-tuple-element.56), channel_id=1, source_target_pairs={{3,2},{7,6},{11,10},{15,14},{19,18},{23,22},{27,26},{31,30}} | collective-permute-start | bytes 614408 | tf_op jit(solution)/shard_map/ppermute | solution.py:445
  65.7 33.9 %copy-start.7 = (bf16[400,256]{1,0:T(8,128)(2,1)S(1)}, bf16[400,256]{1,0:T(8,128)(2,1)}, u32[]{:S(2)}) copy-start(bf16[400,256]{1,0:T(8,128)(2,1)} %get-tuple-element.56) | copy-start | bytes 614404
  94.7 27.1 %collective-permute-start.5 = (bf16[500,400]{1,0:T(8,128)(2,1)}, bf16[500,400]{1,0:T(8,128)(2,1)S(1)}, u32[]{:S(2)}, u32[]{:S(2)}) collective-permute-start(bf16[500,400]{1,0:T(8,128)(2,1)} %pad_maximum_fusion), channel_id=1, source_target_pairs={{0,2},{1,3},{2,0},{3,1},{4,6},{5,7},{6,4},{7,5},{8,10},{9,11},{10,... | collective-permute-start | bytes 1200008 | tf_op jit(solution)/shard_map/ppermute | solution.py:435
  99.6 31.4 %collective-permute-start.3 = (bf16[400,256]{1,0:T(8,128)(2,1)S(1)}, bf16[400,256]{1,0:T(8,128)(2,1)}, u32[]{:S(2)}, u32[]{:S(2)}) collective-permute-start(bf16[400,256]{1,0:T(8,128)(2,1)S(1)} %copy-done.7), channel_id=1, source_target_pairs={{0,1},{1,2},{2,3},{4,5},{5,6},{6,7},{8,9},{9,10},{10,11},{12,13},{... | collective-permute-start | bytes 614408 | tf_op jit(solution)/shard_map/ppermute | solution.py:425
  106.2 182.9 %reduce-scatter.6.cloned.1.call-start = ((), (), s32[]{:S(2)}) async-start(), calls=%async_computation.7 | async-start | bytes 1916928 | tf_op jit(solution)/shard_map/reduce_scatter | solution.py:538
  124.7 2.1 copy-start.3
  126.8 2.7 copy-start.2
  128.3 3.7 copy-start.4
  128.3 2.7 copy-start.8
  220.0 1.0 copy-start.5
  220.0 91.2 %reduce-scatter.4.cloned.1.call-start = ((), (), s32[]{:S(2)}) async-start(), calls=%async_computation.6 | async-start | bytes 3686400 | tf_op jit(solution)/shard_map/reduce_scatter | solution.py:535
  220.8 136.2 %reduce-scatter.8.cloned.1.call-start = ((), (), s32[]{:S(2)}) async-start(), calls=%async_computation.8 | async-start | bytes 2580480 | tf_op jit(solution)/shard_map/reduce_scatter | solution.py:539
  221.1 98.6 %collective-permute-start.10 = (bf16[400,256]{1,0:T(8,128)(2,1)S(1)}, bf16[400,256]{1,0:T(8,128)(2,1)S(1)}, u32[]{:S(2)}, u32[]{:S(2)}) collective-permute-start(bf16[400,256]{1,0:T(8,128)(2,1)S(1)} %convert_element_type.52), channel_id=1, source_target_pairs={{1,0},{2,1},{3,2},{5,4},{6,5},{7,6},{9,8},{10,9},{11,10},{13,12},{... | collective-permute-start | bytes 614408 | tf_op jit(solution)/shard_map/ppermute | solution.py:425
  312.2 7.4 %collective-permute-start.12 = (bf16[400,256]{1,0:T(8,128)(2,1)S(1)}, bf16[400,256]{1,0:T(8,128)(2,1)S(1)}, u32[]{:S(2)}, u32[]{:S(2)}) collective-permute-start(bf16[400,256]{1,0:T(8,128)(2,1)S(1)} %convert_bitcast_fusion), channel_id=1, source_target_pairs={{1,3},{5,7},{9,11},{13,15},{17,19},{21,23},{25,27},{29,31}} | collective-permute-start | bytes 614408 | tf_op jit(solution)/shard_map/ppermute | solution.py:454
  312.9 10.3 %collective-permute-start.11 = (bf16[400,256]{1,0:T(8,128)(2,1)S(1)}, bf16[400,256]{1,0:T(8,128)(2,1)S(1)}, u32[]{:S(2)}, u32[]{:S(2)}) collective-permute-start(bf16[400,256]{1,0:T(8,128)(2,1)S(1)} %convert_bitcast_fusion), channel_id=1, source_target_pairs={{0,3},{4,7},{8,11},{12,15},{16,19},{20,23},{24,27},{28,31}} | collective-permute-start | bytes 614408 | tf_op jit(solution)/shard_map/ppermute | solution.py:454
  318.8 4.4 collective-permute-start.13
  342.0 19.2 %all-to-all-start.1 = ((bf16[8,100,2]{1,2,0:T(2,128)(2,1)}), bf16[8,100,2]{1,2,0:T(2,128)(2,1)S(1)}, u32[]{:S(2)}, u32[]{:S(2)}) async-start(bf16[8,100,2]{1,2,0:T(2,128)(2,1)} %copy.182), calls=%async_computation.4 | async-start | bytes 8192 | tf_op jit(solution)/shard_map/all_to_all | solution.py:566
  361.2 16.3 %all-to-all-start = ((bf16[8,50,803]{2,1,0:T(8,128)(2,1)}), bf16[8,50,803]{2,1,0:T(8,128)(2,1)S(1)}, u32[]{:S(2)}, u32[]{:S(2)}) async-start(bf16[8,50,803]{2,1,0:T(8,128)(2,1)} %convert_element_type.60), calls=%async_computation.3 | async-start | bytes 1605632 | tf_op jit(solution)/shard_map/all_to_all | solution.py:566
  364.8 51.9 %all-gather.8.cloned.1.call-start = ((), (), s32[]{:S(2)}) async-start(), calls=%async_computation.10 | async-start | bytes 1548288 | tf_op jit(solution)/shard_map/all_gather | solution.py:585
  416.6 9.3 %copy-start = (f32[8,50,712]{2,1,0:T(8,128)S(1)}, f32[8,50,712]{2,1,0:T(8,128)}, u32[]{:S(2)}) copy-start(f32[8,50,712]{2,1,0:T(8,128)} %all-gather.8.cloned.1.call-done) | copy-start | bytes 3417604
Sparse Core Ops, SparseCore 0:
  106.3 24.1 all-gather.5
  220.1 40.2 reduce-scatter.5
  264.3 46.8 reduce-scatter.3
  314.8 42.2 reduce-scatter.7
  392.1 24.5 all-gather.7

commit v2 on v1

v2 whole, which is shorter than its diff:
```python
import functools

import jax
import jax.numpy as jnp
from jax import lax
from jax.experimental import pallas as pl
from jax.experimental.pallas import tpu as pltpu
from jax.sharding import PartitionSpec as P

STEP = 16
REACH = 2 * STEP
LANES = 128
GROUP = 4
TILE = 16
epsilon = 1e-05
bf16 = jnp.bfloat16
f32 = jnp.float32
VMEM_BYTES = 58 * 2**20
WHOLE = pl.BlockSpec(memory_space=pltpu.VMEM)
PARAMS = pltpu.CompilerParams(vmem_limit_bytes=VMEM_BYTES)


def cost(flops, moved):
    return pl.CostEstimate(flops=int(2.5 * flops), bytes_accessed=int(moved), transcendentals=0)


def dot(a, b, ca, cb):
    return lax.dot_general(a, b, (((ca,), (cb,)), ((), ())), preferred_element_type=f32)


def at(column):
    return slice(column * LANES, (column + 1) * LANES)


def tiles(depth):
    return [slice(r, r + TILE) for r in range(0, depth, TILE)]


class Columns:
    def __init__(self, ref):
        self.ref = ref
        self.per = ref.shape[-1] // LANES
        self.count = ref.shape[0] * self.per

    def key(self, rows, c):
        return (c // self.per,) + (0,) * (len(self.ref.shape) - 3) + (rows, at(c % self.per))

    def get(self, rows, c):
        return self.ref[self.key(rows, c)].astype(f32)

    def put(self, rows, c, values):
        self.ref[self.key(rows, c)] = values.astype(self.ref.dtype)


ROW = slice(0, 1)


def down(values):
    return jnp.sum(values, axis=0, keepdims=True)


def stats(load, depth, columns):
    zero = jnp.zeros((TILE, LANES), f32)
    sums = [zero] * columns
    for t in tiles(depth):
        sums = [s + load(t, c) for c, s in enumerate(sums)]
    means = [down(s) * (1.0 / depth) for s in sums]
    sums = [zero] * columns
    for t in tiles(depth):
        for c in range(columns):
            center = load(t, c) - means[c]
            sums[c] = sums[c] + center * center
    scales = [lax.rsqrt(down(s) * (1.0 / depth) + epsilon) for s in sums]
    return means, scales


def halved(vec):
    return 0.5 * vec


def backward_pass(columns, depth, normed, g_in, vec, sums, keep, act=None):
    g_gain, g_shift = sums
    zero = jnp.zeros((TILE, LANES), f32)
    totals = [[zero, zero] for _ in range(columns)]
    for t in tiles(depth):
        gain, shift = vec[0, t, :], vec[1, t, :]
        half_gain, half_shift = halved(gain), halved(shift)
        gains = shifts = None
        for c in range(columns):
            n = normed(t, c)
            half = n * half_gain + half_shift
            tan = jnp.tanh(half)
            if act is not None:
                act(t, c, half * tan + half)
            slope = (1.0 + tan) * (1.0 + half * (1.0 - tan))
            g = g_in(t, c) * slope
            gn = g * n
            u = g * gain
            keep(t, c, u)
            totals[c][0] = totals[c][0] + u
            totals[c][1] = totals[c][1] + gn * gain
            gains = gn if gains is None else gains + gn
            shifts = g if shifts is None else shifts + g
        g_gain[t, :] += gains
        g_shift[t, :] += shifts
    return [[down(s) * (1.0 / depth) for s in pair] for pair in totals]


def blocks(shape, lanes, group, first, batch=0):
    full = (group,) + tuple(shape[1:-1]) + (lanes,)
    zeros = (0,) * (len(shape) - 2)
    return pl.BlockSpec(full, lambda i: (i + batch // group,) + zeros + (first // lanes,))


def shape_of(*shape, kind=f32):
    return jax.ShapeDtypeStruct(shape, kind)


def splits(own):
    return 2 if own % 2 == 0 else 1


def sending_kernel(ids, w_in, w_conv_t, w_out, *refs):
    rows, (in_part, rest_part), vecs = refs[:6], refs[6:8], refs[8:]
    own, width = w_out.shape
    inner = w_conv_t.shape[1]
    parts = splits(own)
    few = own // parts
    in_part[...] = w_in[...].astype(bf16)
    conv = [w_conv_t[k].T for k in range(3)]
    for h in range(parts):

        @pl.when(ids[1] % parts == h)
        def _():
            mine = slice(h * few, (h + 1) * few)
            pieces = [turn[mine] for turn in conv]
            pieces += [w_out[mine, q : q + inner] for q in range(0, width, inner)]
            rest_part[...] = jnp.concatenate(pieces, axis=0).astype(bf16)

    for k, row in enumerate(rows):
        wide = jnp.broadcast_to(row[...], (LANES, row.shape[1]))
        vecs[k // 2][k % 2] = wide.T


def sending(ids, w_in, w_conv, w_out, rows):
    own, width = w_out.shape
    inner = w_conv.shape[2]
    parts = splits(own)
    return pl.pallas_call(
        sending_kernel,
        in_specs=[pl.BlockSpec(memory_space=pltpu.SMEM)] + [WHOLE] * 9,
        out_specs=[WHOLE] * 5,
        out_shape=[
            shape_of(*w_in.shape, kind=bf16),
            shape_of((3 + width // inner) * own // parts, inner, kind=bf16),
            shape_of(2, width, LANES),
            shape_of(2, inner, LANES),
            shape_of(2, inner, LANES),
        ],
        compiler_params=PARAMS,
        name="sending",
    )(ids, w_in, jnp.swapaxes(w_conv, 1, 2), w_out, *[row[None] for row in rows])


def with_shift(weights, shift):
    parts = []
    left = shift
    for _ in range(3):
        part = left.astype(bf16).astype(f32)
        parts.append(part)
        left = left - part
    parts.append(jnp.zeros((13, shift.shape[1]), f32))
    return jnp.concatenate([weights.T, jnp.concatenate(parts, axis=0).T], axis=1).astype(bf16)


def taking_in_kernel(ids, pieces, bias, half_in, w_in_t, total):
    shards, some, _ = pieces.shape
    for j in range(shards):
        total[j * some : (j + 1) * some, :] = pieces[ids[0] ^ j].astype(f32)
    half_in[...] = (0.5 * total[...]).astype(bf16)
    w_in_t[...] = with_shift(total[...], bias[...])


def taking_in(ids, pieces, bias):
    shards, some, inner = pieces.shape
    width = shards * some
    return pl.pallas_call(
        taking_in_kernel,
        in_specs=[pl.BlockSpec(memory_space=pltpu.SMEM)] + [WHOLE] * 2,
        out_specs=[WHOLE] * 2,
        out_shape=[shape_of(width, inner, kind=bf16), shape_of(inner, width + 16, kind=bf16)],
        scratch_shapes=[pltpu.VMEM((width, inner), f32)],
        compiler_params=PARAMS,
        name="taking_in",
    )(ids, pieces, bias[None])


def taking_rest_kernel(ids, pieces, bias_conv, bias_out, *refs):
    (w_conv_t, half_conv, w_out_t, half_out), (conv, out) = refs[:4], refs[4:]
    parts, shards, rows, inner = pieces.shape
    width = out.shape[1]
    few = rows // (3 + width // inner)
    for j in range(shards):
        for h in range(parts):
            first = (j * parts + h) * few
            piece = pieces[h ^ (ids[1] % parts), ids[0] ^ j].astype(f32)
            for k in range(3):
                conv[k * inner + first : k * inner + first + few, :] = piece[k * few : (k + 1) * few]
            halves = [piece[k * few : (k + 1) * few] for k in range(3, 3 + width // inner)]
            out[first : first + few, :] = jnp.concatenate(halves, axis=1)
    half_conv[...] = (0.5 * conv[...]).astype(bf16)
    w_conv_t[...] = with_shift(conv[...], bias_conv[...])
    half_out[...] = (0.5 * out[...]).astype(bf16)
    w_out_t[...] = with_shift(out[...], bias_out[...])


def taking_rest(ids, pieces, bias_conv, bias_out):
    inner, width = bias_conv.shape[0], bias_out.shape[0]
    return pl.pallas_call(
        taking_rest_kernel,
        in_specs=[pl.BlockSpec(memory_space=pltpu.SMEM)] + [WHOLE] * 3,
        out_specs=[WHOLE] * 4,
        out_shape=[
            shape_of(inner, 3 * inner + 16, kind=bf16),
            shape_of(3 * inner, inner, kind=bf16),
            shape_of(width, inner + 16, kind=bf16),
            shape_of(inner, width, kind=bf16),
        ],
        scratch_shapes=[pltpu.VMEM((3 * inner, inner), f32), pltpu.VMEM((inner, width), f32)],
        compiler_params=PARAMS,
        name="taking_rest",
    )(ids, pieces, bias_conv[None], bias_out[None])


def lead_kernel(*refs):
    x_refs, vec1, outs = refs[:2], refs[2], refs[3:]
    for s in range(2):
        x, act, mean, scale = (Columns(ref) for ref in (x_refs[s],) + tuple(outs[3 * s : 3 * s + 3]))
        depth = x_refs[s].shape[-2]
        means, scales = stats(x.get, depth, x.count)
        for c in range(x.count):
            mean.put(ROW, c, means[c])
            scale.put(ROW, c, scales[c])
        shifts = [m * v for m, v in zip(means, scales)]
        for t in tiles(depth):
            gain, shift = halved(vec1[0, t, :]), halved(vec1[1, t, :])
            for c in range(x.count):
                half = (x.get(t, c) * scales[c] - shifts[c]) * gain + shift
                act.put(t, c, half * jnp.tanh(half) + half)
        for c in range(x.count):
            act.put(slice(depth, depth + 16), c, jnp.ones((16, LANES), f32))


def lead(xs, vec1):
    batches, _, width, _ = xs[0].shape
    in_specs, out_specs, out_shape = [], [], []
    for x in xs:
        lanes = x.shape[3]
        in_specs.append(blocks(x.shape, lanes, 1, 0))
        for depth, kind in ((width + 16, bf16), (1, f32), (1, f32)):
            out_specs.append(blocks((batches, depth, lanes), lanes, 1, 0))
            out_shape.append(shape_of(batches, depth, lanes, kind=kind))
    return pl.pallas_call(
        lead_kernel,
        grid=(batches,),
        in_specs=in_specs + [WHOLE],
        out_specs=out_specs,
        out_shape=out_shape,
        compiler_params=PARAMS,
        cost_estimate=cost(0, sum(x.size for x in xs) * 4),
        name="lead",
    )(*xs, vec1)


def front_kernel(streams, with_rim, *refs):
    acts, refs = refs[:streams], refs[streams:]
    (w_in_t, vec2), refs = refs[:2], refs[2:]
    outs, refs = [refs[3 * s : 3 * s + 3] for s in range(streams)], refs[3 * streams :]
    rim_ref = refs[0] if with_rim else None
    hiddens = refs[-streams:]
    inner = w_in_t.shape[0]
    for s in range(streams):
        act, hidden = acts[s], hiddens[s]
        mid, n2, r2 = (Columns(ref) for ref in outs[s])
        wide = act.shape[2]
        for q in range(act.shape[0]):
            hidden[:, q * wide : (q + 1) * wide] = dot(w_in_t[...], act[q], 1, 0)
        load = lambda t, c: hidden[t, at(c)]
        means, scales = stats(load, inner, mid.count)
        shifts = [m * v for m, v in zip(means, scales)]
        for c in range(mid.count):
            r2.put(ROW, c, scales[c])
        for t in tiles(inner):
            gain, shift = halved(vec2[0, t, :]), halved(vec2[1, t, :])
            rim = []
            for c in range(mid.count):
                n = load(t, c) * scales[c] - shifts[c]
                half = n * gain + shift
                value = half * jnp.tanh(half) + half
                mid.put(t, c, value)
                n2.put(t, c, n)
                rim.append(value[:, LANES - REACH :])
            if with_rim:
                rim_ref[t, :] = jnp.concatenate(rim, axis=1).astype(bf16)


def front(acts, parts, w_in_t, vec2, with_rim=False):
    inner = w_in_t.shape[0]
    batches = acts[0].shape[0]
    in_specs, out_specs, out_shape, scratch = [], [], [], []
    for act, (lanes, group, first) in zip(acts, parts):
        in_specs.append(blocks(act.shape, lanes, group, first))
        for depth, kind in ((inner, bf16), (inner, bf16), (1, f32)):
            out_specs.append(blocks((batches, depth, lanes), lanes, group, 0))
            out_shape.append(shape_of(batches, depth, lanes, kind=kind))
        scratch.append(pltpu.VMEM((inner, group * lanes), f32))
    if with_rim:
        out_specs.append(pl.BlockSpec((inner, GROUP * REACH), lambda i: (0, i)))
        out_shape.append(shape_of(inner, batches * REACH, kind=bf16))
    return pl.pallas_call(
        functools.partial(front_kernel, len(acts), with_rim),
        grid=(batches // parts[0][1],),
        in_specs=in_specs + [WHOLE] * 2,
        out_specs=out_specs,
        out_shape=out_shape,
        scratch_shapes=scratch,
        compiler_params=PARAMS,
        cost_estimate=cost(4 * w_in_t.size * sum(batches * part[0] for part in parts), 0),
        name="front",
    )(*acts, w_in_t, vec2)


def shifted_right(values, by):
    zeros = jnp.zeros((values.shape[0], by), values.dtype)
    return jnp.concatenate([zeros, values[:, : values.shape[1] - by]], axis=1)


def shifted_left(values, by):
    zeros = jnp.zeros((values.shape[0], by), values.dtype)
    return jnp.concatenate([values[:, by:], zeros], axis=1)


def chosen(base, position, fits, batches):
    one = jnp.where(jnp.logical_and(fits, position < STEP), base + STEP + position, -1)
    two = jnp.where(jnp.logical_and(fits, position < REACH), base + position, -1)
    target = jnp.concatenate([one, two], axis=1)
    row = lax.broadcasted_iota(jnp.int32, (batches * REACH, target.shape[1]), 0)
    return jnp.where(row == target, 1.0, 0.0).astype(bf16)


def middle_kernel(batches, prompts, group, pieces, has_before, has_after, *refs):
    if not prompts:
        (cont_start, cont_map), refs = refs[:2], refs[2:]
    mids, refs = refs[:pieces], refs[pieces:]
    (x_ref, cot_ref, tails), refs = refs[:3], refs[3:]
    (w_conv_t, w_conv, w_out_t, w_out, vec3), refs = refs[:5], refs[5:]
    if has_before:
        before, refs = refs[:4], refs[4:]
    out_ref, gs, refs = refs[0], refs[1 : 1 + pieces], refs[1 + pieces :]
    sums, table_out, refs = refs[:4], refs[4], refs[5:]
    table, refs = refs[-1], refs[:-1]
    if has_after:
        chunks, refs = refs[0], refs[1:]
    gw_out, gw_conv, g_gain3, g_shift3 = sums
    taps, act, gc, gt, conv, g_act, cots = refs
    width = w_out_t.shape[0]
    inner = w_out.shape[0]
    step = pl.program_id(0)
    length = taps.shape[1] // group
    columns = taps.shape[1] // LANES

    @pl.when(step == 0)
    def _():
        for k, ref in enumerate(sums):
            ref[...] = before[k][...] if has_before else jnp.zeros_like(ref)
        table[...] = jnp.zeros_like(table)
        taps[3 * inner :, :] = jnp.ones_like(taps[3 * inner :, :])
        act[inner:, :] = jnp.ones_like(act[inner:, :])

    reads = []
    for q in range(group):
        m = step * group + q
        base = m * REACH
        here = q * length
        span = slice(here, here + length)
        start_span = slice(here, here + LANES)
        cots[:, span] = cot_ref[q, 0]
        mid = mids[0][q] if pieces == 1 else jnp.concatenate([ref[q] for ref in mids], axis=1)
        lane = lax.broadcasted_iota(jnp.int32, (1, LANES), 1)
        if prompts:
            begin = chosen(base, lane, lane >= 0, batches)
            before_rows = tails[...]
            reads.append((begin,))
        else:
            start = cont_start[m, 0, 1]
            owners = cont_map[m, 0, 0], cont_map[m, 0, 1]
            at_most = (length // LANES - 2) * LANES
            window = jnp.minimum(lax.shift_right_logical(start, 7) * LANES, at_most)
            wide = pl.ds(pl.multiple_of(here + window, LANES), 2 * LANES)
            begin = chosen(base, lane, lane < start, batches)
            before_rows = tails[owners[0]]
        first = dot(before_rows, begin, 1, 0).astype(bf16)
        taps[0:inner, span] = mid
        one, two = shifted_right(mid, STEP), shifted_right(mid, REACH)
        if not prompts:
            row = lax.broadcasted_iota(jnp.int32, (1, length), 1)
            since = jnp.where(row < start, row, row - start)
            near_one = jnp.where(since >= STEP, 1.0, 0.0)
            near_two = jnp.where(since >= REACH, 1.0, 0.0)
            full = lambda w: jnp.broadcast_to(w, (inner, length)).astype(bf16)
            one, two = one * full(near_one), two * full(near_two)
        taps[inner : 2 * inner, span] = one
        taps[2 * inner : 3 * inner, span] = two
        taps[inner : 2 * inner, start_span] += first[:, :LANES]
        taps[2 * inner : 3 * inner, start_span] += first[:, LANES:]
        if not prompts:
            offset = window + lax.broadcasted_iota(jnp.int32, (1, 2 * LANES), 1) - start
            later = chosen(base, offset, offset >= 0, batches)
            far = dot(tails[owners[1]], later, 1, 0).astype(bf16)
            taps[inner : 2 * inner, wide] += far[:, : 2 * LANES]
            taps[2 * inner : 3 * inner, wide] += far[:, 2 * LANES :]
            reads.append((begin, owners, wide, later, near_one, near_two))
    conv[...] = dot(w_conv_t[...], taps[...], 1, 0)
    g_act[...] = dot(w_out[...], cots[...], 1, 0)
    load = lambda t, c: conv[t, at(c)]
    means, scales = stats(load, inner, columns)
    shifts = [a * b for a, b in zip(means, scales)]

    def keep(t, c, u):
        g_act[t, at(c)] = u

    def put_act(t, c, value):
        act[t, at(c)] = value.astype(bf16)

    totals = backward_pass(
        columns,
        inner,
        lambda t, c: load(t, c) * scales[c] - shifts[c],
        lambda t, c: g_act[t, at(c)],
        vec3,
        (g_gain3, g_shift3),
        keep,
        put_act,
    )
    for c in range(columns):
        mean_u, mean_un = totals[c]
        by_x = -(scales[c] * scales[c] * mean_un)
        constant = -(scales[c] * mean_u) - means[c] * by_x
        for t in tiles(inner):
            g_in = g_act[t, at(c)] * scales[c] + (load(t, c) * by_x + constant)
            gc[t, at(c)] = g_in.astype(bf16)
    branch = dot(w_out_t[...], act[...], 1, 0)
    for q in range(group):
        span = slice(q * length, (q + 1) * length)
        out_ref[q, 0] = (x_ref[q, 0].astype(f32) + branch[:, span]).astype(bf16)
    gw_out[...] += dot(cots[...], act[...], 1, 1)
    gw_conv[...] += dot(gc[...], taps[...], 1, 1)
    g_taps = dot(w_conv[...], gc[...], 1, 0)
    for q in range(group):
        span = slice(q * length, (q + 1) * length)
        g0, g1, g2 = (g_taps[k * inner : (k + 1) * inner, span] for k in range(3))
        both = jnp.concatenate([g1[:, :LANES], g2[:, :LANES]], axis=1).astype(bf16)
        back = dot(both, reads[q][0], 1, 1)
        if prompts:
            table[...] += back
        else:
            begin, owners, wide, later, near_one, near_two = reads[q]
            table[owners[0]] += back
            gt[0, :, span] = g1.astype(bf16)
            gt[1, :, span] = g2.astype(bf16)
            both = jnp.concatenate([gt[0, :, wide], gt[1, :, wide]], axis=1)
            table[owners[1]] += dot(both, later, 1, 1)
            g1, g2 = g1 * near_one, g2 * near_two
        g_mid = (g0 + shifted_left(g1, STEP) + shifted_left(g2, REACH)).astype(bf16)
        if pieces == 1:
            gs[0][q] = g_mid
        else:
            gs[0][q] = g_mid[:, : length - LANES]
            gs[1][q] = g_mid[:, length - LANES :]

    @pl.when(step == pl.num_programs(0) - 1)
    def _():
        table_out[...] = table[...].astype(bf16)
        if has_after:
            count, few, _ = chunks.shape
            gw_conv[:, 3 * inner + 1 : 3 * inner + 2] = jnp.sum(g_gain3[...], axis=1, keepdims=True)
            gw_conv[:, 3 * inner + 2 : 3 * inner + 3] = jnp.sum(g_shift3[...], axis=1, keepdims=True)
            twice = width // inner
            for r in range(count):
                parts = [gw_conv[r * few : (r + 1) * few, : 3 * inner + 3]]
                for h in range(r * twice, (r + 1) * twice):
                    parts.append(gw_out[h * few : (h + 1) * few, : inner + 1])
                chunks[r] = jnp.concatenate(parts, axis=1).astype(bf16)


def middle(prompts, group, scalars, mids, x, cot, tails, weights, before=None, chunks=0):
    batches, _, width, length = x.shape
    inner = mids[0].shape[1]
    block = lambda a: blocks(a.shape, a.shape[-1], group, 0)
    args = list(scalars) + mids + [x, cot, tails] + list(weights) + list(before or ())
    in_specs = [pl.BlockSpec(memory_space=pltpu.SMEM)] * len(scalars)
    in_specs += [block(a) for a in mids + [x, cot]]
    in_specs += [WHOLE] * (len(args) - len(in_specs))
    out_like = [shape_of(*x.shape, kind=bf16)]
    out_like += [shape_of(*mid.shape, kind=bf16) for mid in mids]
    sums = [
        shape_of(width, inner + 16),
        shape_of(inner, 3 * inner + 16),
        shape_of(inner, LANES),
        shape_of(inner, LANES),
        shape_of(*tails.shape, kind=bf16),
    ]
    if chunks:
        wide = 3 * inner + 3 + (width // inner) * (inner + 1)
        sums.append(shape_of(chunks, inner // chunks, wide, kind=bf16))
    total = group * length
    scratch = [
        pltpu.VMEM((3 * inner + 16, total), bf16),
        pltpu.VMEM((inner + 16, total), bf16),
        pltpu.VMEM((inner, total), bf16),
        pltpu.VMEM((2, inner, total), bf16),
        pltpu.VMEM((inner, total), f32),
        pltpu.VMEM((inner, total), f32),
        pltpu.VMEM((width, total), bf16),
    ]
    scratch.append(pltpu.VMEM(tails.shape, f32))
    return pl.pallas_call(
        functools.partial(
            middle_kernel, batches, prompts, group, len(mids), before is not None, chunks > 0
        ),
        grid=(batches // group,),
        in_specs=in_specs,
        out_specs=[block(a) for a in out_like] + [WHOLE] * len(sums),
        out_shape=out_like + sums,
        scratch_shapes=scratch,
        compiler_params=PARAMS,
        cost_estimate=cost(batches * length * 9 * inner * width, 3 * x.size * 2),
        name="middle",
    )(*args)


def inner_back_kernel(has_rim, has_before, has_after, *refs):
    (act_ref, g_ref, n2_ref, r2_ref, vec2), refs = refs[:5], refs[5:]
    if has_rim:
        rim, refs = refs[0], refs[1:]
    if has_before:
        before, refs = refs[:3], refs[3:]
    gh_ref, sums, refs = refs[0], refs[1:4], refs[4:]
    if has_after:
        in_chunks, refs = refs[0], refs[1:]
    (kept,) = refs
    gw_in, g_gain2, g_shift2 = sums
    inner = vec2.shape[1]
    step = pl.program_id(0)

    @pl.when(step == 0)
    def _():
        for k, ref in enumerate(sums):
            ref[...] = before[k][...] if has_before else jnp.zeros_like(ref)

    g, n2, r2, gh = (Columns(ref) for ref in (g_ref, n2_ref, r2_ref, gh_ref))

    def g_in(t, c):
        value = g.get(t, c)
        if has_rim:
            piece = rim[t, c * REACH : (c + 1) * REACH]
            value += jnp.concatenate([jnp.zeros((TILE, LANES - REACH), f32), piece], axis=1)
        return value

    def keep(t, c, u):
        kept[t, at(c)] = u

    totals = backward_pass(g.count, inner, n2.get, g_in, vec2, (g_gain2, g_shift2), keep)
    for c in range(g.count):
        mean_u, mean_un = totals[c]
        scale = r2.get(ROW, c)
        by_n, constant = -(scale * mean_un), -(scale * mean_u)
        for t in tiles(inner):
            gh.put(t, c, kept[t, at(c)] * scale + (n2.get(t, c) * by_n + constant))
    for q in range(act_ref.shape[0]):
        gw_in[...] += dot(gh_ref[q], act_ref[q], 1, 1)

    if has_after:

        @pl.when(step == pl.num_programs(0) - 1)
        def _():
            count, few, wide = in_chunks.shape
            gw_in[:, wide - 2 : wide - 1] = jnp.sum(g_gain2[...], axis=1, keepdims=True)
            gw_in[:, wide - 1 : wide] = jnp.sum(g_shift2[...], axis=1, keepdims=True)
            for r in range(count):
                in_chunks[r] = gw_in[r * few : (r + 1) * few, :wide].astype(bf16)


def inner_back(act, g, n2, r2, part, vec2, rim=None, before=None, chunks=0):
    inner = vec2.shape[1]
    batches, width = act.shape[0], act.shape[1] - 16
    lanes, group, first = part
    in_specs = [blocks(act.shape, lanes, group, first)]
    in_specs += [blocks(a.shape, lanes, group, 0) for a in (g, n2, r2)] + [WHOLE]
    args = [act, g, n2, r2, vec2]
    if rim is not None:
        args.append(rim)
        in_specs.append(pl.BlockSpec((inner, GROUP * REACH), lambda i: (0, i)))
    if before is not None:
        args += before
        in_specs += [WHOLE] * 3
    sums = [shape_of(inner, width + 16), shape_of(inner, LANES), shape_of(inner, LANES)]
    if chunks:
        sums.append(shape_of(chunks, inner // chunks, width + 3, kind=bf16))
    return pl.pallas_call(
        functools.partial(inner_back_kernel, rim is not None, before is not None, chunks > 0),
        grid=(batches // group,),
        in_specs=in_specs,
        out_specs=[blocks(g.shape, lanes, group, 0)] + [WHOLE] * len(sums),
        out_shape=[shape_of(*g.shape, kind=bf16)] + sums,
        scratch_shapes=[pltpu.VMEM((inner, group * lanes), f32)],
        compiler_params=PARAMS,
        cost_estimate=cost(4 * width * inner * batches * lanes, 0),
        name="inner_back",
    )(*args)


def outer_back_kernel(pieces, has_before, has_into, has_after, *refs):
    (x_ref, cot_ref, mean_ref, scale_ref), refs = refs[:4], refs[4:]
    ghs, refs = refs[:pieces], refs[pieces:]
    (w_in, vec1), refs = refs[:2], refs[2:]
    if has_before:
        before, refs = refs[:2], refs[2:]
    if has_into:
        refs = refs[1:]
    out_ref, sums, refs = refs[0], refs[1:3], refs[3:]
    if has_after:
        small, refs = refs[0], refs[1:]
    (g_act,) = refs
    width = w_in.shape[0]
    step = pl.program_id(0)

    @pl.when(step == 0)
    def _():
        for k, ref in enumerate(sums):
            ref[...] = before[k][...] if has_before else jnp.zeros_like(ref)

    first = 0
    for gh in ghs:
        length = gh.shape[-1]
        g_act[:, first : first + length] = dot(w_in[...], gh[0], 1, 0)
        first += length
    x, cot, mean, scale, out = (Columns(r) for r in (x_ref, cot_ref, mean_ref, scale_ref, out_ref))
    scales = [scale.get(ROW, c) for c in range(x.count)]
    means = [mean.get(ROW, c) for c in range(x.count)]
    shifts = [a * b for a, b in zip(means, scales)]

    def keep(t, c, u):
        g_act[t, at(c)] = u

    totals = backward_pass(
        x.count,
        width,
        lambda t, c: x.get(t, c) * scales[c] - shifts[c],
        lambda t, c: g_act[t, at(c)],
        vec1,
        sums,
        keep,
    )
    for c in range(x.count):
        mean_u, mean_un = totals[c]
        by_x = -(scales[c] * scales[c] * mean_un)
        constant = -(scales[c] * mean_u) - means[c] * by_x
        for t in tiles(width):
            change = g_act[t, at(c)] * scales[c] + (x.get(t, c) * by_x + constant)
            out.put(t, c, cot.get(t, c) + change)

    if has_after:

        @pl.when(step == pl.num_programs(0) - 1)
        def _():
            for k in range(2):
                small[:, k * width : (k + 1) * width] = down(sums[k][...].T)


def outer_back(
    x, cot, mean, scale, ghs, w_in, vec1, batches, before=None, into=None, last=False
):
    first, count = batches
    width, lanes = x.shape[2:]
    block = lambda a: blocks(a.shape, a.shape[-1], 1, 0, first)
    args = [x, cot, mean, scale] + ghs
    in_specs = [block(a) for a in args] + [WHOLE] * 2
    args += [w_in, vec1]
    if before is not None:
        args += before
        in_specs += [WHOLE] * 2
    aliases = {}
    if into is not None:
        aliases = {len(args): 0}
        args.append(into)
        in_specs.append(pl.BlockSpec(memory_space=pl.ANY))
    sums = [shape_of(width, LANES), shape_of(width, LANES)]
    if last:
        sums.append(shape_of(1, 2 * width))
    return pl.pallas_call(
        functools.partial(
            outer_back_kernel, len(ghs), before is not None, into is not None, last
        ),
        grid=(count,),
        in_specs=in_specs,
        out_specs=[block(x)] + [WHOLE] * len(sums),
        out_shape=[shape_of(*x.shape)] + sums,
        scratch_shapes=[pltpu.VMEM((width, lanes), f32)],
        input_output_aliases=aliases,
        compiler_params=PARAMS,
        cost_estimate=cost(8 * w_in.size * count * lanes, 0),
        name="outer_back",
    )(*args)


def packing_kernel(inner, ids, early_ref, late_ref, *refs):
    pieces, packed = refs[:-1], refs[-1]
    total = lambda ref: jnp.sum(ref[...].astype(f32), axis=0)
    early, late = total(early_ref), total(late_ref)
    shards = len(pieces)
    width = late.shape[1] - 3
    own, wide = inner // shards, width // shards
    conv_end = 3 * inner + 3
    firsts = range(conv_end, early.shape[1], inner + 1)
    kept = [early[:, first + inner : first + inner + 1] for first in firsts]
    kept += [early[:, 3 * inner : conv_end], late[:, width:]]
    starts = list(firsts) + [k * inner for k in range(3)]
    for j in range(shards):
        parts = [early[:, first + j * own : first + (j + 1) * own] for first in starts]
        parts += [late[:, j * wide : (j + 1) * wide]]
        packed[ids[0] ^ j] = jnp.concatenate(parts + kept, axis=1)
    for k in range(shards):
        pieces[k][...] = packed[k].astype(pieces[k].dtype)


def packing(ids, shards, inner, early, late):
    few, width = early.shape[1], late.shape[2] - 3
    wide = (2 * width + 3 * inner) // shards + width // inner + 6
    kinds = [f32] + [bf16] * (shards - 1)
    return pl.pallas_call(
        functools.partial(packing_kernel, inner),
        in_specs=[pl.BlockSpec(memory_space=pltpu.SMEM)] + [WHOLE] * 2,
        out_specs=[WHOLE] * shards,
        out_shape=[shape_of(few, wide, kind=kind) for kind in kinds],
        scratch_shapes=[pltpu.VMEM((shards, few, wide), f32)],
        compiler_params=PARAMS,
        name="packing",
    )(ids, early, late)


def unpacking_kernel(whole, by_out, by_conv, by_in, by_width, by_inner, tall, tall_in):
    reps, few, _ = whole.shape
    own, width = by_out.shape
    inner = by_conv.shape[1]
    wide = by_in.shape[0]
    twice = width // inner
    first_in = (twice + 3) * own
    small = first_in + wide
    for r in range(reps):
        piece = whole[r].astype(f32)
        for h in range(twice):
            rows = slice((r * twice + h) * few, (r * twice + h + 1) * few)
            tall[rows, :own] = piece[:, h * own : (h + 1) * own]
            tall[rows, own : own + 1] = piece[:, small + h : small + h + 1]
        rows = slice(r * few, (r + 1) * few)
        for k in range(3):
            by_conv[k, rows, :] = piece[:, (twice + k) * own : (twice + k + 1) * own]
        tall_in[rows, :wide] = piece[:, first_in : first_in + wide]
        tall_in[rows, wide : wide + 6] = piece[:, small + twice : small + twice + 6]
    turned = tall[...].T
    by_out[...] = turned[:own]
    by_width[...] = turned[own : own + 1]
    turned = tall_in[...].T
    by_in[...] = turned[:wide]
    by_inner[...] = turned[wide : wide + 6]


def unpacking(whole, shards, inner, width):
    own, wide = inner // shards, width // shards
    up = lambda n: -(-n // LANES) * LANES
    return pl.pallas_call(
        unpacking_kernel,
        in_specs=[WHOLE],
        out_specs=[WHOLE] * 5,
        out_shape=[
            shape_of(own, width),
            shape_of(3, inner, own),
            shape_of(wide, inner),
            shape_of(1, width),
            shape_of(6, inner),
        ],
        scratch_shapes=[
            pltpu.VMEM((width, up(own + 1)), f32),
            pltpu.VMEM((inner, up(wide + 6)), f32),
        ],
        compiler_params=PARAMS,
        name="unpacking",
    )(whole)


def passed_along(x, axis, by):
    size = lax.axis_size(axis)
    pairs = [(i, i + by) for i in range(size) if 0 <= i + by < size]
    return lax.ppermute(x, axis, pairs)


def swapped(x, axis, k):
    return lax.ppermute(x, axis, [(i, i ^ k) for i in range(lax.axis_size(axis))])


def gathered(x):
    size = lax.axis_size("shard")
    return jnp.stack([x] + [swapped(x, "shard", k) for k in range(1, size)])


def after(value, *others):
    return lax.optimization_barrier((value,) + others)[0]


def sent_from_last(x, axis):
    size = lax.axis_size(axis)
    me = lax.axis_index(axis)
    value = x
    for j in range(size - 1):
        piece = lax.ppermute(x, axis, [(size - 1, j)])
        value = jnp.where(me == j, piece, value)
    return value


def summed_at_last(x, axis):
    size = lax.axis_size(axis)
    total = x.astype(f32)
    for j in range(size - 1):
        total = total + lax.ppermute(x, axis, [(j, size - 1)]).astype(f32)
    return total


def dealt(x, axis):
    return lax.all_to_all(x, axis, 0, 0, tiled=True)


def summed_everywhere(x):
    x = jnp.sum(lax.optimization_barrier(lax.all_gather(x, "rep")), axis=0)
    size = lax.axis_size("shard")
    if size > 4:
        return lax.psum(x, "shard")
    return x + sum(swapped(x, "shard", k) for k in range(1, size))


def on_device(
    prompt_x,
    cont_x,
    cont_map,
    cont_start,
    w_in,
    w_conv,
    w_out,
    norm1_gain,
    norm1_bias,
    bias_in,
    norm2_gain,
    norm2_bias,
    bias_conv,
    norm3_gain,
    norm3_bias,
    bias_out,
    prompt_cot,
    cont_cot,
):
    inner = w_conv.shape[2]
    turned = lambda a: jnp.swapaxes(a, 2, 3)
    prompt_x, cont_x, prompt_cot, cont_cot = map(turned, (prompt_x, cont_x, prompt_cot, cont_cot))
    width = prompt_x.shape[2]
    shards, reps = lax.axis_size("shard"), lax.axis_size("rep")
    is_last = lax.axis_index("shard") == shards - 1
    own = w_out.shape[0]
    parts = splits(own)
    ids = jnp.stack([lax.axis_index("shard"), lax.axis_index("rep") % 2]).astype(jnp.int32)
    rows = (norm1_gain, norm1_bias, norm2_gain, norm2_bias, norm3_gain, norm3_bias)
    in_part, rest_part, vec1, vec2, vec3 = sending(ids, w_in, w_conv, w_out, rows)
    rows_p, rows_c = prompt_x.shape[3], cont_x.shape[3]
    last = (LANES, GROUP, rows_p - LANES)
    rest = (rows_p - LANES, 1, 0)
    every = (rows_c, 1, 0)
    have_first = rows_p > LANES
    act_p, mean_p, scale_p, act_c, mean_c, scale_c = lead([prompt_x, cont_x], vec1)
    in_pieces, rest_part, act_p = lax.optimization_barrier((gathered(in_part), rest_part, act_p))
    half_in, w_in_t = taking_in(ids, in_pieces, bias_in)
    rest_pieces = gathered(rest_part)
    mid_l, n2_l, r2_l, rim = front([act_p], [last], w_in_t, vec2, with_rim=True)
    halo = passed_along(rim, "shard", 1)
    own_tail = sent_from_last(rim, "shard")
    mids = [mid_l]
    if have_first:
        mid_f, n2_f, r2_f = front([act_p], [rest], w_in_t, vec2)
        mids = [mid_f, mid_l]
    rest_pieces, act_c, _ = lax.optimization_barrier((rest_pieces, act_c, mids[0]))
    if parts == 2:
        rest_pieces = jnp.stack([rest_pieces, swapped(rest_pieces, "rep", 1)])
    else:
        rest_pieces = rest_pieces[None]
    mid_c, n2_c, r2_c = front([act_c], [every], w_in_t, vec2)
    rest_pieces, own_tail, mid_c = lax.optimization_barrier((rest_pieces, own_tail, mid_c))
    tails = lax.all_gather(own_tail, "rep", axis=0)

    weights = (*taking_rest(ids, rest_pieces, bias_conv, bias_out), vec3)
    prompt_out, *results = middle(True, 1, [], mids, prompt_x, prompt_cot, halo, weights)
    g_ps, results = results[: len(mids)], results[len(mids) :]
    sums, rim_out = results[:4], results[4]
    back_rim = passed_along(rim_out, "shard", -1)
    cont_out, g_c, *results = middle(
        False,
        1,
        [cont_start, cont_map],
        [mid_c],
        cont_x,
        cont_cot,
        tails,
        weights,
        before=sums,
        chunks=reps,
    )
    table, early = results[4:]
    table = dealt(table, "rep")

    sums = None
    gh_ps = []
    if have_first:
        gh_f, *sums = inner_back(act_p, g_ps[0], n2_f, r2_f, rest, vec2)
        gh_ps.append(gh_f)
    gh_c, *sums = inner_back(act_c, g_c, n2_c, r2_c, every, vec2, before=sums)
    table, gh_c = lax.optimization_barrier((table, gh_c))
    own_tail = jnp.sum(table.astype(f32), axis=0).astype(bf16)
    own_tail, early = lax.optimization_barrier((own_tail, early))
    own_tail = summed_at_last(own_tail, "shard")
    early = dealt(early, "rep")
    batches = prompt_x.shape[0]
    one, two = (0, batches // 2), (batches // 2, batches // 2)
    outer_c = functools.partial(
        outer_back, cont_x, cont_cot, mean_c, scale_c, [gh_c], half_in, vec1
    )
    cont_grad, *sums1 = outer_c(one)
    cont_grad, own_tail = lax.optimization_barrier((cont_grad, own_tail))
    rim_in = back_rim.astype(f32) + jnp.where(is_last, own_tail, 0.0)
    gh_l, *results = inner_back(
        act_p, g_ps[-1], n2_l, r2_l, last, vec2, rim=rim_in, before=sums, chunks=reps
    )
    late, early, gh_l = lax.optimization_barrier((results[3], early, gh_l))
    late = dealt(late, "rep")
    gh_ps.append(gh_l)
    cont_grad, *sums1 = outer_c(two, before=sums1, into=after(cont_grad, gh_l))
    late, cont_grad = lax.optimization_barrier((late, cont_grad))

    mine, *others = packing(ids, shards, inner, early, late)
    others = [swapped(other, "shard", k + 1) for k, other in enumerate(others)]
    outer_p = functools.partial(
        outer_back, prompt_x, prompt_cot, mean_p, scale_p, gh_ps, half_in, vec1
    )
    prompt_grad, *sums1 = outer_p(one, before=[after(sums1[0], mine), sums1[1]])
    *others, prompt_grad = lax.optimization_barrier((*others, prompt_grad))
    mine = mine + sum(other.astype(f32) for other in others)
    whole = lax.all_gather(mine, "rep")
    prompt_grad, *results = outer_p(two, before=sums1, into=after(prompt_grad, mine), last=True)
    ones = summed_everywhere(results[2])[0]
    whole = after(whole, ones)
    grad_w_out, grad_w_conv, grad_w_in, grad_bias_out, small = unpacking(whole, shards, inner, width)
    grad_bias_conv, grad_gain3, grad_shift3, grad_bias_in, grad_gain2, grad_shift2 = small
    return (
        turned(prompt_out),
        turned(cont_out),
        turned(prompt_grad),
        turned(cont_grad),
        grad_w_in,
        jnp.swapaxes(grad_w_conv, 1, 2),
        grad_w_out,
        ones[:width],
        ones[width:],
        grad_bias_in,
        grad_gain2,
        grad_shift2,
        grad_bias_conv,
        grad_gain3,
        grad_shift3,
        grad_bias_out[0],
    )


def solution(mesh):
    rows = P(None, "rep", "shard", None)
    buffers = P(None, ("rep", "shard"), None, None)
    in_specs = (
        rows,
        buffers,
        P(None, ("rep", "shard"), None),
        P(None, ("rep", "shard"), None),
        P("shard", None),
        P(None, "shard", None),
        P("shard", None),
    ) + (P(),) * 9 + (rows, buffers)
    out_specs = (
        rows,
        buffers,
        rows,
        buffers,
        P("shard", None),
        P(None, "shard", None),
        P("shard", None),
    ) + (P(),) * 9
    return jax.shard_map(
        on_device, mesh=mesh, in_specs=in_specs, out_specs=out_specs, check_vma=False
    )
```

time: 446 us -> 331 us (0.74)
  waiting for transfers between devices: 115 us -> 13.6 us
  local copies, waits for them, and re-layouts: 41.5 us -> 8.66 us
  Pallas kernels: 204 us -> 227 us
  other arithmetic: 11.9 us -> 7.32 us
    reduce_scatter x3 -> x0, waiting for transfers between devices: 32.7 us -> none  [the longest x1 21 us: on_device(): own_tail = lax.psum_scatter(table, 'rep', scatter_dimension=0)]
    ppermute x6 -> x13, waiting for transfers between devices: 41.5 us -> 10.1 us  [swapped(): lax.ppermute(x, axis, [(i, i ^ k) for i in range(lax.axis_size(axis))])]
    pallas_call x5 -> x16, Pallas kernels: 117 us -> 143 us  [the longest x4 48.5 us: outer_back(): pl.pallas_call(functools.partial(outer_back_kernel, len(ghs), before is n...]
    all_gather x1, waiting for transfers between devices: 24.7 us -> 0.01 us  [on_device(): whole = lax.all_gather(mine, 'rep')]
    all_to_all x1 -> x0, blocking collectives: 12.7 us -> none  [on_device(): lax.all_to_all(a.astype(bf16), axis, 0, 0, tiled=True).astype(f32)]
    all_gather x0 -> x1, blocking collectives: none -> 9.35 us  [summed_everywhere(): x = jnp.sum(lax.optimization_barrier(lax.all_gather(x, 'rep')), axis=0)]
    all_to_all x2 -> x3, waiting for transfers between devices: 12.2 us -> 3.48 us  [dealt(): return lax.all_to_all(x, axis, 0, 0, tiled=True)]
    slice x14 -> x1, local copies, waits for them, and re-layouts: 7.85 us -> 0.68 us  [on_device(): ones[width:]]
  transfers between devices with their start and end apart: 21 -> 26, of which waited for: 8 -> 6; matrix products, arithmetic and copies ran while one was open for 7% -> 2% of each run, Pallas kernels for 36% -> 67%
where the time goes in v2:
time: 331 us; the launch traced here: 325 us
  Pallas kernels  227 us (69%)
  starting transfers between devices  43.3 us (13%)
  between operations  14.9 us (5%)
  waiting for transfers between devices  13.6 us (4%)
  blocking collectives  9.35 us (3%)
  local copies, waits for them, and re-layouts  8.66 us (3%)
  other arithmetic  7.32 us (2%)
    pallas_call x2, Pallas kernels, middle(): pl.pallas_call(functools.partial(middle_kernel, batches, prompts, group,...  84.7 us
    pallas_call x4, Pallas kernels, outer_back(): pl.pallas_call(functools.partial(outer_back_kernel, len(ghs), before is n...  48.5 us
    pallas_call x3, Pallas kernels, inner_back(): pl.pallas_call(functools.partial(inner_back_kernel, rim is not None, befo...  33.3 us
    pallas_call x3, Pallas kernels, front(): pl.pallas_call(functools.partial(front_kernel, len(acts), with_rim), grid...  27.7 us
    ppermute x13, starting transfers between devices, swapped(): lax.ppermute(x, axis, [(i, i ^ k) for i in range(lax.axis_size(axis))])  18.9 us
    pallas_call x1, Pallas kernels, lead(): pl.pallas_call(lead_kernel, grid=(batches,), in_specs=in_specs + [WHOLE],...  16.5 us
    all_to_all x3, starting transfers between devices, dealt(): return lax.all_to_all(x, axis, 0, 0, tiled=True)  11.8 us
    ppermute x13, waiting for transfers between devices, swapped(): lax.ppermute(x, axis, [(i, i ^ k) for i in range(lax.axis_size(axis))])  10.1 us
  transfers between devices with their start and end apart: 26, of which 6 were waited for; matrix products, arithmetic and copies ran while one was open for 2% of the time, Pallas kernels for 67%

profile of v2, /device:TPU:0, one launch (start us, length us, event | category | flops | bytes accessed | tf_op | source)
XLA Modules:
  0.0 324.6 jit_solution(15923786226092073316)
XLA Ops:
  7.2 1.3 broadcast_in_dim.31.refs_0_
  8.5 1.3 broadcast_in_dim.32.refs_1_
  10.4 3.2 sending.1
  13.5 5.0 %collective-permute-start.2 = (bf16[200,400]{1,0:T(8,128)(2,1)}, bf16[200,400]{1,0:T(8,128)(2,1)S(1)}, u32[]{:S(2)}, u32[]{:S(2)}) collective-permute-start(bf16[200,400]{1,0:T(8,128)(2,1)} %get-tuple-element.111), channel_id=1, source_target_pairs={{0,3},{1,2},{2,1},{3,0},{4,7},{5,6},{6,5},{7,4},{8,11},{9,10},{10,... | collective-permute-start | bytes 480008 | tf_op jit(solution)/shard_map/ppermute | solution.py:809
  19.2 16.5 %lead.1 = (bf16[8,816,512]{2,1,0:T(8,128)(2,1)}, f32[8,1,512]{2,1,0:T(1,128)}, f32[8,1,512]{2,1,0:T(1,128)}, bf16[8,816,512]{2,1,0:T(8,128)(2,1)}, f32[8,1,512]{2,1,0:T(1,128)}, /*index=5*/f32[8,1,512]{2,1,0:T(1,128)}) custom-call(bf16[8,1,800,512]{3,2,1,0:T(8,128)(2,1)} %bitcast.42, bf16[8,1,800,512]{3,2,1,0:T(8,128)(2,1)} %bitcast.38, ...), custom_call_target="tpu_custom_call" | custom-call | bytes 26214400 | tf_op jit(solution)/shard_map/lead/pallas_call | solution.py:263
  36.2 1.0 pad_maximum_fusion.2.pieces
  37.2 3.4 %collective-permute-start.6 = (bf16[250,400]{1,0:T(8,128)(2,1)S(1)}, bf16[250,400]{1,0:T(8,128)(2,1)S(1)}, u32[]{:S(2)}, u32[]{:S(2)}) collective-permute-start(bf16[250,400]{1,0:T(8,128)(2,1)S(1)} %copy-done.2), channel_id=1, source_target_pairs={{0,3},{1,2},{2,1},{3,0},{4,7},{5,6},{6,5},{7,4},{8,11},{9,10},{10,... | collective-permute-start | bytes 600008 | tf_op jit(solution)/shard_map/ppermute | solution.py:809
  40.6 1.0 collective-permute-start.4
  41.6 2.6 taking_in.1
  44.2 5.2 %front.4 = (bf16[8,400,128]{2,1,0:T(8,128)(2,1)}, bf16[8,400,128]{2,1,0:T(8,128)(2,1)}, f32[8,1,128]{2,1,0:T(1,128)}, bf16[400,256]{1,0:T(8,128)(2,1)}) custom-call(bf16[8,816,512]{2,1,0:T(8,128)(2,1)} %get-tuple-element.115.refs_0_, bf16[400,816]{1,0:T(8,128)(2,1)} %get-tuple-element.117.refs_1_, f32[2,400,128]{2,1,0:T(8,128)} %get-tuple-element.118.refs_2_.refs_4_), custom_call_target="tpu_custom_call" | custom-call | flops 3342336000 | tf_op jit(solution)/shard_map/front/pallas_call | solution.py:320
  49.4 1.4 collective-permute-start.10
  50.8 0.7 collective-permute-start.9
  51.5 10.6 %front.3 = (bf16[8,400,384]{2,1,0:T(8,128)(2,1)}, bf16[8,400,384]{2,1,0:T(8,128)(2,1)}, f32[8,1,384]{2,1,0:T(1,128)}) custom-call(bf16[8,816,512]{2,1,0:T(8,128)(2,1)} %get-tuple-element.115.refs_0_, bf16[400,816]{1,0:T(8,128)(2,1)} %get-tuple-element.117.refs_1_, f32[2,400,128]{2,1,0:T(8,128)} %get-tuple-element.118.refs_2_.refs_4_), custom_call_target="tpu_custom_call" | custom-call | flops 10027008000 | tf_op jit(solution)/shard_map/front/pallas_call | solution.py:320
  62.1 0.7 collective-permute-start.8
  62.8 8.0 %collective-permute-done.5 = bf16[250,400]{1,0:T(8,128)(2,1)S(1)} collective-permute-done((bf16[250,400]{1,0:T(8,128)(2,1)S(1)}, bf16[250,400]{1,0:T(8,128)(2,1)S(1)}, u32[]{:S(2)}, u32[]{:S(2)}) %collective-permute-start.5) | collective-permute-done | bytes 200032 | tf_op jit(solution)/shard_map/ppermute | solution.py:809
  70.8 2.1 collective-permute-start.3
  73.7 11.9 %front.5 = (bf16[8,400,512]{2,1,0:T(8,128)(2,1)}, bf16[8,400,512]{2,1,0:T(8,128)(2,1)}, f32[8,1,512]{2,1,0:T(1,128)}) custom-call(bf16[8,816,512]{2,1,0:T(8,128)(2,1)} %get-tuple-element.125.refs_0_, bf16[400,816]{1,0:T(8,128)(2,1)} %get-tuple-element.117.refs_1_, f32[2,400,128]{2,1,0:T(8,128)} %get-tuple-element.118.refs_2_.refs_4_), custom_call_target="tpu_custom_call" | custom-call | flops 13369344000 | tf_op jit(solution)/shard_map/front/pallas_call | solution.py:320
  85.7 0.7 select_select_fusion
  87.0 1.6 pad_maximum_fusion.pieces
  90.5 4.6 %taking_rest.1 = (bf16[400,1216]{1,0:T(8,128)(2,1)}, bf16[1200,400]{1,0:T(8,128)(2,1)}, bf16[800,416]{1,0:T(8,128)(2,1)}, bf16[400,800]{1,0:T(8,128)(2,1)}) custom-call(s32[2]{0:T(128)} %pad_add_fusion.ids, bf16[2,4,250,400]{3,2,1,0:T(8,128)(2,1)} %pad_maximum_fusion.pieces, f32[1,400]{1,0:T(1,128)} %bitcast.63, f32[1,800]{1,0:T(1,128)} %broadcast_in_dim.39.bias_out), custom_call_target="tpu_custom_call" | custom-call | tf_op jit(solution)/shard_map/taking_rest/pallas_call | solution.py:219
  95.2 39.1 %middle.2 = (bf16[8,1,800,512]{3,2,1,0:T(8,128)(2,1)}, bf16[8,400,384]{2,1,0:T(8,128)(2,1)}, bf16[8,400,128]{2,1,0:T(8,128)(2,1)}, f32[800,416]{1,0:T(8,128)}, f...) custom-call(bf16[8,400,384]{2,1,0:T(8,128)(2,1)} %get-tuple-element.119.refs_0_, ...), custom_call_target="tpu_custom_call" | custom-call | flops 29491200000 | bytes 19660800 | tf_op jit(solution)/shard_map/middle/pallas_call | solution.py:527
  134.2 1.5 collective-permute-start.11
  135.8 45.7 %middle.3 = (bf16[8,1,800,512]{3,2,1,0:T(8,128)(2,1)}, bf16[8,400,512]{2,1,0:T(8,128)(2,1)}, f32[800,416]{1,0:T(8,128)}, f32[400,1216]{1,0:T(8,128)}, f32[400,12...) custom-call(s32[8,1,2]{2,1,0:T(1,128)} %copy.40.refs_0_, ...), custom_call_target="tpu_custom_call" | custom-call | flops 29491200000 | bytes 19660800 | tf_op jit(solution)/shard_map/middle/pallas_call | solution.py:527
  181.4 3.8 %all-to-all-start = ((bf16[8,400,256]{2,1,0:T(8,128)(2,1)}), bf16[8,400,256]{2,1,0:T(8,128)(2,1)S(1)}, u32[]{:S(2)}, u32[]{:S(2)}) async-start(bf16[8,400,256]{2,1,0:T(8,128)(2,1)} %get-tuple-element.153), calls=%async_computation | async-start | bytes 3276800 | tf_op jit(solution)/shard_map/all_to_all | solution.py:840
  185.2 11.8 %inner_back.3 = (bf16[8,400,384]{2,1,0:T(8,128)(2,1)}, f32[400,816]{1,0:T(8,128)}, f32[400,128]{1,0:T(8,128)}, f32[400,128]{1,0:T(8,128)}) custom-call(bf16[8,816,512]{2,1,0:T(8,128)(2,1)} %get-tuple-element.115.refs_0_, bf16[8,400,384]{2,1,0:T(8,128)(2,1)} %get-tuple-element.143.refs_1_, bf16[8,400,384]{2,1,0:T(8,128)(2,1)} %get-tuple-element.144.refs_2_, ...), custom_call_target="tpu_custom_call" | custom-call | flops 9830400000 | tf_op jit(solution)/shard_map/inner_back/pallas_call | solution.py:610
  197.0 13.8 %inner_back.4 = (bf16[8,400,512]{2,1,0:T(8,128)(2,1)}, f32[400,816]{1,0:T(8,128)}, f32[400,128]{1,0:T(8,128)}, f32[400,128]{1,0:T(8,128)}) custom-call(bf16[8,816,512]{2,1,0:T(8,128)(2,1)} %get-tuple-element.125.refs_0_, bf16[8,400,512]{2,1,0:T(8,128)(2,1)} %get-tuple-element.154.refs_1_, bf16[8,400,512]{2,1,0:T(8,128)(2,1)} %get-tuple-element.155.refs_2_, ...), custom_call_target="tpu_custom_call" | custom-call | flops 13107200000 | tf_op jit(solution)/shard_map/inner_back/pallas_call | solution.py:610
  211.8 0.7 collective-permute-start.13
  212.5 4.7 %collective-permute-start.12 = (bf16[400,256]{1,0:T(8,128)(2,1)S(1)}, bf16[400,256]{1,0:T(8,128)(2,1)S(1)}, u32[]{:S(2)}, u32[]{:S(2)}) collective-permute-start(bf16[400,256]{1,0:T(8,128)(2,1)S(1)} %reduce_sum.23), channel_id=1, source_target_pairs={{0,3},{4,7},{8,11},{12,15},{16,19},{20,23},{24,27},{28,31}} | collective-permute-start | bytes 614408 | tf_op jit(solution)/shard_map/ppermute | solution.py:835
  217.2 4.5 %all-to-all-start.1 = ((bf16[8,50,2005]{2,1,0:T(8,128)(2,1)}), bf16[8,50,2005]{2,1,0:T(8,128)(2,1)S(1)}, u32[]{:S(2)}, u32[]{:S(2)}) async-start(bf16[8,50,2005]{2,1,0:T(8,128)(2,1)} %get-tuple-element.172), calls=%async_computation.1 | async-start | bytes 3670016 | tf_op jit(solution)/shard_map/all_to_all | solution.py:840
  221.7 12.0 %outer_back.4 = (f32[8,1,800,512]{3,2,1,0:T(8,128)}, f32[800,128]{1,0:T(8,128)}, f32[800,128]{1,0:T(8,128)}) custom-call(bf16[8,1,800,512]{3,2,1,0:T(8,128)(2,1)} %bitcast.40, bf16[8,1,800,512]{3,2,1,0:T(8,128)(2,1)} %bitcast.71, f32[8,1,512]{2,1,0:T(1,128)} %get-tuple-element.151.refs_2_, f32[8,1,512]{2,1,0:T(1,128)} %get-tuple-element.152.refs_3_, ...), custom_call_target="tpu_custom_call" | custom-call | flops 13107200000 | tf_op jit(solution)/shard_map/outer_back/pallas_call | solution.py:701
  233.9 0.8 select_add_fusion.refs_5_
  234.7 7.7 %inner_back.5 = (bf16[8,400,128]{2,1,0:T(8,128)(2,1)}, f32[400,816]{1,0:T(8,128)}, f32[400,128]{1,0:T(8,128)}, f32[400,128]{1,0:T(8,128)}, bf16[8,50,803]{2,1,0:T(8,128)(2,1)}) custom-call(bf16[8,816,512]{2,1,0:T(8,128)(2,1)} %get-tuple-element.115.refs_0_, bf16[8,400,128]{2,1,0:T(8,128)(2,1)} %get-tuple-element.147.refs_1_, ...), custom_call_target="tpu_custom_call" | custom-call | flops 3276800000 | tf_op jit(solution)/shard_map/inner_back/pallas_call | solution.py:610
  242.4 3.1 all-to-all-done.1.early_ref
  245.5 3.5 %all-to-all-start.2 = ((bf16[8,50,803]{2,1,0:T(8,128)(2,1)}), bf16[8,50,803]{2,1,0:T(8,128)(2,1)S(1)}, u32[]{:S(2)}, u32[]{:S(2)}) async-start(bf16[8,50,803]{2,1,0:T(8,128)(2,1)} %get-tuple-element.181), calls=%async_computation.2 | async-start | bytes 1605632 | tf_op jit(solution)/shard_map/all_to_all | solution.py:840
  249.1 12.3 %outer_back.5 = (f32[8,1,800,512]{3,2,1,0:T(8,128)}, f32[800,128]{1,0:T(8,128)}, f32[800,128]{1,0:T(8,128)}) custom-call(bf16[8,1,800,512]{3,2,1,0:T(8,128)(2,1)} %bitcast.41, bf16[8,1,800,512]{3,2,1,0:T(8,128)(2,1)} %bitcast.72, f32[8,1,512]{2,1,0:T(1,128)} %get-tuple-element.151.refs_2_, ...), custom_call_target="tpu_custom_call", output_to_operand_aliasing={{0}: (9, {})} | custom-call | flops 13107200000 | tf_op jit(solution)/shard_map/outer_back/pallas_call | solution.py:701
  261.8 0.9 copy-done.1
  262.6 3.0 packing.1
  265.7 4.3 %collective-permute-start.17 = (bf16[50,708]{1,0:T(8,128)(2,1)}, bf16[50,708]{1,0:T(8,128)(2,1)S(1)}, u32[]{:S(2)}, u32[]{:S(2)}) collective-permute-start(bf16[50,708]{1,0:T(8,128)(2,1)} %get-tuple-element.191), channel_id=1, source_target_pairs={{0,3},{1,2},{2,1},{3,0},{4,7},{5,6},{6,5},{7,4},{8,11},{9,10},{10,... | collective-permute-start | bytes 212408 | tf_op jit(solution)/shard_map/ppermute | solution.py:809
  270.1 12.2 %outer_back.6 = (f32[8,1,800,512]{3,2,1,0:T(8,128)}, f32[800,128]{1,0:T(8,128)}, f32[800,128]{1,0:T(8,128)}) custom-call(bf16[8,1,800,512]{3,2,1,0:T(8,128)(2,1)} %bitcast.44, bf16[8,1,800,512]{3,2,1,0:T(8,128)(2,1)} %bitcast.74, f32[8,1,512]{2,1,0:T(1,128)} %get-tuple-element.141.refs_2_, f32[8,1,512]{2,1,0:T(1,128)} %get-tuple-element.142.refs_3_, ...), custom_call_target="tpu_custom_call" | custom-call | flops 13107200000 | tf_op jit(solution)/shard_map/outer_back/pallas_call | solution.py:701
  282.3 0.7 add_add_fusion
  283.0 12.0 %outer_back.7 = (f32[8,1,800,512]{3,2,1,0:T(8,128)}, f32[800,128]{1,0:T(8,128)}, f32[800,128]{1,0:T(8,128)}, f32[1,1600]{1,0:T(1,128)}) custom-call(bf16[8,1,800,512]{3,2,1,0:T(8,128)(2,1)} %bitcast.45, bf16[8,1,800,512]{3,2,1,0:T(8,128)(2,1)} %bitcast.75, f32[8,1,512]{2,1,0:T(1,128)} %get-tuple-element.141.refs_2_, ...), custom_call_target="tpu_custom_call", output_to_operand_aliasing={{0}: (10, {})} | custom-call | flops 13107200000 | tf_op jit(solution)/shard_map/outer_back/pallas_call | solution.py:701
  295.1 9.4 %all-gather.4 = f32[8,1,1600]{2,1,0:T(1,128)S(1)} all-gather(f32[1,1,1600]{2,1,0:T(1,128)} %bitcast.57), channel_id=4, replica_groups=mesh['rep'=8,'shard'=4] {'rep'}, dimensions={0}, use_global_device_ids=true | all-gather | bytes 57600 | tf_op jit(solution)/shard_map/all_gather | solution.py:844
  305.2 3.8 %collective-permute-start.18 = (f32[1,1600]{1,0:T(1,128)S(1)}, f32[1,1600]{1,0:T(1,128)S(1)}, u32[]{:S(2)}, u32[]{:S(2)}) collective-permute-start(f32[1,1600]{1,0:T(1,128)S(1)} %reduce_sum.25), channel_id=1, source_target_pairs={{0,1},{1,0},{2,3},{3,2},{4,5},{5,4},{6,7},{7,6},{8,9},{9,8},{10,11... | collective-permute-start | bytes 19208 | tf_op jit(solution)/shard_map/ppermute | solution.py:809
  309.0 1.0 collective-permute-done.20
  310.6 0.7 slice_reduce_fusion
  311.3 3.2 unpacking.1
  314.5 1.5 fusion
  316.0 1.3 reduce.4
  (65 shorter events, 7.8 us)
Async XLA Ops:
  7.2 128.6 %all-gather.8.cloned.1.call-start = ((), (), s32[]{:S(2)}) async-start(), calls=%async_computation.3 | async-start | bytes 1843200 | tf_op jit(solution)/shard_map/all_gather | solution.py:905
  13.5 22.2 %collective-permute-start.2 = (bf16[200,400]{1,0:T(8,128)(2,1)}, bf16[200,400]{1,0:T(8,128)(2,1)S(1)}, u32[]{:S(2)}, u32[]{:S(2)}) collective-permute-start(bf16[200,400]{1,0:T(8,128)(2,1)} %get-tuple-element.111), channel_id=1, source_target_pairs={{0,3},{1,2},{2,1},{3,0},{4,7},{5,6},{6,5},{7,4},{8,11},{9,10},{10,... | collective-permute-start | bytes 480008 | tf_op jit(solution)/shard_map/ppermute | solution.py:809
  18.6 17.6 %collective-permute-start.1 = (bf16[200,400]{1,0:T(8,128)(2,1)}, bf16[200,400]{1,0:T(8,128)(2,1)S(1)}, u32[]{:S(2)}, u32[]{:S(2)}) collective-permute-start(bf16[200,400]{1,0:T(8,128)(2,1)} %get-tuple-element.111), channel_id=1, source_target_pairs={{0,2},{1,3},{2,0},{3,1},{4,6},{5,7},{6,4},{7,5},{8,10},{9,11},{10,... | collective-permute-start | bytes 480008 | tf_op jit(solution)/shard_map/ppermute | solution.py:809
  18.6 17.6 %collective-permute-start = (bf16[200,400]{1,0:T(8,128)(2,1)}, bf16[200,400]{1,0:T(8,128)(2,1)S(1)}, u32[]{:S(2)}, u32[]{:S(2)}) collective-permute-start(bf16[200,400]{1,0:T(8,128)(2,1)} %get-tuple-element.111), channel_id=1, source_target_pairs={{0,1},{1,0},{2,3},{3,2},{4,5},{5,4},{6,7},{7,6},{8,9},{9,8},{10,11... | collective-permute-start | bytes 480008 | tf_op jit(solution)/shard_map/ppermute | solution.py:809
  19.2 17.0 %copy-start.3 = (bf16[200,400]{1,0:T(8,128)(2,1)S(1)}, bf16[200,400]{1,0:T(8,128)(2,1)}, u32[]{:S(2)}) copy-start(bf16[200,400]{1,0:T(8,128)(2,1)} %get-tuple-element.111) | copy-start | bytes 480004
  19.2 18.1 %copy-start.2 = (bf16[250,400]{1,0:T(8,128)(2,1)S(1)}, bf16[250,400]{1,0:T(8,128)(2,1)}, u32[]{:S(2)}) copy-start(bf16[250,400]{1,0:T(8,128)(2,1)} %get-tuple-element.122) | copy-start | bytes 600004
  37.2 24.9 %collective-permute-start.6 = (bf16[250,400]{1,0:T(8,128)(2,1)S(1)}, bf16[250,400]{1,0:T(8,128)(2,1)S(1)}, u32[]{:S(2)}, u32[]{:S(2)}) collective-permute-start(bf16[250,400]{1,0:T(8,128)(2,1)S(1)} %copy-done.2), channel_id=1, source_target_pairs={{0,3},{1,2},{2,1},{3,0},{4,7},{5,6},{6,5},{7,4},{8,11},{9,10},{10,... | collective-permute-start | bytes 600008 | tf_op jit(solution)/shard_map/ppermute | solution.py:809
  40.6 30.2 %collective-permute-start.5 = (bf16[250,400]{1,0:T(8,128)(2,1)S(1)}, bf16[250,400]{1,0:T(8,128)(2,1)S(1)}, u32[]{:S(2)}, u32[]{:S(2)}) collective-permute-start(bf16[250,400]{1,0:T(8,128)(2,1)S(1)} %copy-done.2), channel_id=1, source_target_pairs={{0,2},{1,3},{2,0},{3,1},{4,6},{5,7},{6,4},{7,5},{8,10},{9,11},{10,... | collective-permute-start | bytes 600008 | tf_op jit(solution)/shard_map/ppermute | solution.py:809
  40.6 32.3 %collective-permute-start.4 = (bf16[250,400]{1,0:T(8,128)(2,1)S(1)}, bf16[250,400]{1,0:T(8,128)(2,1)S(1)}, u32[]{:S(2)}, u32[]{:S(2)}) collective-permute-start(bf16[250,400]{1,0:T(8,128)(2,1)S(1)} %copy-done.2), channel_id=1, source_target_pairs={{0,1},{1,0},{2,3},{3,2},{4,5},{5,4},{6,7},{7,6},{8,9},{9,8},{10,11... | collective-permute-start | bytes 600008 | tf_op jit(solution)/shard_map/ppermute | solution.py:809
  49.4 12.8 %copy-start.4 = (bf16[400,256]{1,0:T(8,128)(2,1)S(1)}, bf16[400,256]{1,0:T(8,128)(2,1)}, u32[]{:S(2)}) copy-start(bf16[400,256]{1,0:T(8,128)(2,1)} %get-tuple-element.121) | copy-start | bytes 614404
  49.4 36.3 %collective-permute-start.10 = (bf16[400,256]{1,0:T(8,128)(2,1)}, bf16[400,256]{1,0:T(8,128)(2,1)S(1)}, u32[]{:S(2)}, u32[]{:S(2)}) collective-permute-start(bf16[400,256]{1,0:T(8,128)(2,1)} %get-tuple-element.121), channel_id=1, source_target_pairs={{3,0},{7,4},{11,8},{15,12},{19,16},{23,20},{27,24},{31,28}} | collective-permute-start | bytes 614408 | tf_op jit(solution)/shard_map/ppermute | solution.py:826
  50.8 34.9 %collective-permute-start.9 = (bf16[400,256]{1,0:T(8,128)(2,1)}, bf16[400,256]{1,0:T(8,128)(2,1)S(1)}, u32[]{:S(2)}, u32[]{:S(2)}) collective-permute-start(bf16[400,256]{1,0:T(8,128)(2,1)} %get-tuple-element.121), channel_id=1, source_target_pairs={{3,1},{7,5},{11,9},{15,13},{19,17},{23,21},{27,25},{31,29}} | collective-permute-start | bytes 614408 | tf_op jit(solution)/shard_map/ppermute | solution.py:826
  62.1 23.6 %collective-permute-start.8 = (bf16[400,256]{1,0:T(8,128)(2,1)S(1)}, bf16[400,256]{1,0:T(8,128)(2,1)S(1)}, u32[]{:S(2)}, u32[]{:S(2)}) collective-permute-start(bf16[400,256]{1,0:T(8,128)(2,1)S(1)} %copy-done.4), channel_id=1, source_target_pairs={{3,2},{7,6},{11,10},{15,14},{19,18},{23,22},{27,26},{31,30}} | collective-permute-start | bytes 614408 | tf_op jit(solution)/shard_map/ppermute | solution.py:826
  70.8 24.4 %collective-permute-start.3 = (bf16[400,256]{1,0:T(8,128)(2,1)S(1)}, bf16[400,256]{1,0:T(8,128)(2,1)}, u32[]{:S(2)}, u32[]{:S(2)}) collective-permute-start(bf16[400,256]{1,0:T(8,128)(2,1)S(1)} %copy-done.4), channel_id=1, source_target_pairs={{0,1},{1,2},{2,3},{4,5},{5,6},{6,7},{8,9},{9,10},{10,11},{12,13},{... | collective-permute-start | bytes 614408 | tf_op jit(solution)/shard_map/ppermute | solution.py:805
  73.7 12.8 %collective-permute-start.7 = (bf16[4,250,400]{1,2,0:T(8,128)(2,1)S(1)}, bf16[4,250,400]{1,2,0:T(8,128)(2,1)S(1)}, u32[]{:S(2)}, u32[]{:S(2)}) collective-permute-start(bf16[4,250,400]{1,2,0:T(8,128)(2,1)S(1)} %copy.38), channel_id=1, source_target_pairs={{0,4},{4,0},{8,12},{12,8},{16,20},{20,16},{24,28},{28,24},{1,5},{5... | collective-permute-start | bytes 2400008 | tf_op jit(solution)/shard_map/ppermute | solution.py:809
  87.0 1.6 copy-start.6
  87.0 2.2 copy-start.7
  87.0 2.9 copy-start.8
  134.2 99.6 %collective-permute-start.11 = (bf16[400,256]{1,0:T(8,128)(2,1)}, bf16[400,256]{1,0:T(8,128)(2,1)S(1)}, u32[]{:S(2)}, u32[]{:S(2)}) collective-permute-start(bf16[400,256]{1,0:T(8,128)(2,1)} %get-tuple-element.150), channel_id=1, source_target_pairs={{1,0},{2,1},{3,2},{5,4},{6,5},{7,6},{9,8},{10,9},{11,10},{13,12},{... | collective-permute-start | bytes 614408 | tf_op jit(solution)/shard_map/ppermute | solution.py:805
  181.4 29.4 %all-to-all-start = ((bf16[8,400,256]{2,1,0:T(8,128)(2,1)}), bf16[8,400,256]{2,1,0:T(8,128)(2,1)S(1)}, u32[]{:S(2)}, u32[]{:S(2)}) async-start(bf16[8,400,256]{2,1,0:T(8,128)(2,1)} %get-tuple-element.153), calls=%async_computation | async-start | bytes 3276800 | tf_op jit(solution)/shard_map/all_to_all | solution.py:840
  211.1 22.6 %collective-permute-start.14 = (bf16[400,256]{1,0:T(8,128)(2,1)S(1)}, bf16[400,256]{1,0:T(8,128)(2,1)S(1)}, u32[]{:S(2)}, u32[]{:S(2)}) collective-permute-start(bf16[400,256]{1,0:T(8,128)(2,1)S(1)} %reduce_sum.23), channel_id=1, source_target_pairs={{2,3},{6,7},{10,11},{14,15},{18,19},{22,23},{26,27},{30,31}} | collective-permute-start | bytes 614408 | tf_op jit(solution)/shard_map/ppermute | solution.py:835
  211.8 22.0 %collective-permute-start.13 = (bf16[400,256]{1,0:T(8,128)(2,1)S(1)}, bf16[400,256]{1,0:T(8,128)(2,1)S(1)}, u32[]{:S(2)}, u32[]{:S(2)}) collective-permute-start(bf16[400,256]{1,0:T(8,128)(2,1)S(1)} %reduce_sum.23), channel_id=1, source_target_pairs={{1,3},{5,7},{9,11},{13,15},{17,19},{21,23},{25,27},{29,31}} | collective-permute-start | bytes 614408 | tf_op jit(solution)/shard_map/ppermute | solution.py:835
  212.5 21.3 %collective-permute-start.12 = (bf16[400,256]{1,0:T(8,128)(2,1)S(1)}, bf16[400,256]{1,0:T(8,128)(2,1)S(1)}, u32[]{:S(2)}, u32[]{:S(2)}) collective-permute-start(bf16[400,256]{1,0:T(8,128)(2,1)S(1)} %reduce_sum.23), channel_id=1, source_target_pairs={{0,3},{4,7},{8,11},{12,15},{16,19},{20,23},{24,27},{28,31}} | collective-permute-start | bytes 614408 | tf_op jit(solution)/shard_map/ppermute | solution.py:835
  217.2 28.3 %all-to-all-start.1 = ((bf16[8,50,2005]{2,1,0:T(8,128)(2,1)}), bf16[8,50,2005]{2,1,0:T(8,128)(2,1)S(1)}, u32[]{:S(2)}, u32[]{:S(2)}) async-start(bf16[8,50,2005]{2,1,0:T(8,128)(2,1)} %get-tuple-element.172), calls=%async_computation.1 | async-start | bytes 3670016 | tf_op jit(solution)/shard_map/all_to_all | solution.py:840
  245.5 15.9 %copy-start = (bf16[8,50,2005]{2,1,0:T(8,128)(2,1)}, bf16[8,50,2005]{2,1,0:T(8,128)(2,1)S(1)}, u32[]{:S(2)}) copy-start(bf16[8,50,2005]{2,1,0:T(8,128)(2,1)S(1)} %all-to-all-done.1.early_ref) | copy-start | bytes 4812004
  245.5 16.3 %all-to-all-start.2 = ((bf16[8,50,803]{2,1,0:T(8,128)(2,1)}), bf16[8,50,803]{2,1,0:T(8,128)(2,1)S(1)}, u32[]{:S(2)}, u32[]{:S(2)}) async-start(bf16[8,50,803]{2,1,0:T(8,128)(2,1)} %get-tuple-element.181), calls=%async_computation.2 | async-start | bytes 1605632 | tf_op jit(solution)/shard_map/all_to_all | solution.py:840
  249.0 62.2 %all-gather.10.cloned.1.call-start = ((), (), s32[]{:S(2)}) async-start(), calls=%async_computation.4 | async-start | bytes 1548288 | tf_op jit(solution)/shard_map/all_gather | solution.py:963
  261.8 0.9 copy-start.1
  265.7 16.6 %collective-permute-start.15 = (bf16[50,708]{1,0:T(8,128)(2,1)}, bf16[50,708]{1,0:T(8,128)(2,1)S(1)}, u32[]{:S(2)}, u32[]{:S(2)}) collective-permute-start(bf16[50,708]{1,0:T(8,128)(2,1)} %get-tuple-element.189), channel_id=1, source_target_pairs={{0,1},{1,0},{2,3},{3,2},{4,5},{5,4},{6,7},{7,6},{8,9},{9,8},{10,11... | collective-permute-start | bytes 212408 | tf_op jit(solution)/shard_map/ppermute | solution.py:809
  265.7 16.6 %collective-permute-start.16 = (bf16[50,708]{1,0:T(8,128)(2,1)}, bf16[50,708]{1,0:T(8,128)(2,1)S(1)}, u32[]{:S(2)}, u32[]{:S(2)}) collective-permute-start(bf16[50,708]{1,0:T(8,128)(2,1)} %get-tuple-element.190), channel_id=1, source_target_pairs={{0,2},{1,3},{2,0},{3,1},{4,6},{5,7},{6,4},{7,5},{8,10},{9,11},{10,... | collective-permute-start | bytes 212408 | tf_op jit(solution)/shard_map/ppermute | solution.py:809
  265.7 16.5 %collective-permute-start.17 = (bf16[50,708]{1,0:T(8,128)(2,1)}, bf16[50,708]{1,0:T(8,128)(2,1)S(1)}, u32[]{:S(2)}, u32[]{:S(2)}) collective-permute-start(bf16[50,708]{1,0:T(8,128)(2,1)} %get-tuple-element.191), channel_id=1, source_target_pairs={{0,3},{1,2},{2,1},{3,0},{4,7},{5,6},{6,5},{7,4},{8,11},{9,10},{10,... | collective-permute-start | bytes 212408 | tf_op jit(solution)/shard_map/ppermute | solution.py:809
  270.1 12.2 %copy-start.5 = (f32[50,708]{1,0:T(8,128)S(1)}, f32[50,708]{1,0:T(8,128)}, u32[]{:S(2)}) copy-start(f32[50,708]{1,0:T(8,128)} %get-tuple-element.184) | copy-start | bytes 424804
  304.5 5.5 %collective-permute-start.20 = (f32[1,1600]{1,0:T(1,128)S(1)}, f32[1,1600]{1,0:T(1,128)S(1)}, u32[]{:S(2)}, u32[]{:S(2)}) collective-permute-start(f32[1,1600]{1,0:T(1,128)S(1)} %reduce_sum.25), channel_id=1, source_target_pairs={{0,3},{1,2},{2,1},{3,0},{4,7},{5,6},{6,5},{7,4},{8,11},{9,10},{10,... | collective-permute-start | bytes 19208 | tf_op jit(solution)/shard_map/ppermute | solution.py:809
  304.6 5.4 %collective-permute-start.19 = (f32[1,1600]{1,0:T(1,128)S(1)}, f32[1,1600]{1,0:T(1,128)S(1)}, u32[]{:S(2)}, u32[]{:S(2)}) collective-permute-start(f32[1,1600]{1,0:T(1,128)S(1)} %reduce_sum.25), channel_id=1, source_target_pairs={{0,2},{1,3},{2,0},{3,1},{4,6},{5,7},{6,4},{7,5},{8,10},{9,11},{10,... | collective-permute-start | bytes 19208 | tf_op jit(solution)/shard_map/ppermute | solution.py:809
  305.2 5.4 %collective-permute-start.18 = (f32[1,1600]{1,0:T(1,128)S(1)}, f32[1,1600]{1,0:T(1,128)S(1)}, u32[]{:S(2)}, u32[]{:S(2)}) collective-permute-start(f32[1,1600]{1,0:T(1,128)S(1)} %reduce_sum.25), channel_id=1, source_target_pairs={{0,1},{1,0},{2,3},{3,2},{4,5},{5,4},{6,7},{7,6},{8,9},{9,8},{10,11... | collective-permute-start | bytes 19208 | tf_op jit(solution)/shard_map/ppermute | solution.py:809
Sparse Core Ops, SparseCore 0:
  88.7 24.3 all-gather.7
  283.2 23.2 all-gather.9
